TPU v7x, 256 devices: a whole 4x4x8 slice. The times are simulated.
256 devices in a mesh: row: 16 (over y, z_hi), col: 16 (over z_lo, x, core).
Axes of the slice: x: 4, y: 4, z: 8 (z_hi: 4, z_lo: 2; z = z_hi * 2 + z_lo), core: 2. Of those that a mesh axis runs over, the one named last changes fastest.
Arguments:
- trail_adj: float32 [16384, 16384], P('row', 'col'), may hold values from -8.5 to 8.5
- panel: float32 [16384, 256], P(('row', 'col')), may hold values from -0.046875 to 0.046875
- panel_adj: float32 [16384, 256], P(('row', 'col')), may hold values from -6 to 6
- diag_inverse: float32 [256, 256], replicated, may hold values from -3 to 2, as said below
- corner_adj: float32 [256, 256], replicated, may hold values from -6 to 6
Outputs:
- solved_adj: float32 [16384, 256], P(('row', 'col'))
- corner: float32 [256, 256], replicated
Inputs may be any that keep to these rules, and one draw needn't show every extreme that they name: `diag_inverse`: lower triangular, its diagonal between 1 and 2.
All inputs are finite; a program needn't handle non-finite values.
Results may differ from a plain program's by a relative error of at most 0.00007.
Values sent between devices are 32-bit elements; how exact they have to be, the bound alone decides.
A program may use at most 64 MiB of HBM per device.

v0:
```python
import jax
import jax.numpy as jnp
from jax import lax
from jax.sharding import PartitionSpec as P


def body(trail_adj, panel, panel_adj, diag_inverse, corner_adj):
    highest = lax.Precision.HIGHEST
    row_count = lax.axis_size("row")
    column_index = lax.axis_index("col")
    own_rows = panel.shape[0]
    block_cols = own_rows * row_count
    whole = lax.all_gather(panel, ("row", "col"), axis=0, tiled=True)
    col_block = lax.dynamic_slice_in_dim(whole, column_index * block_cols, block_cols, 0)
    reduced = lax.psum_scatter(
        jnp.dot(trail_adj, col_block, precision=highest, preferred_element_type=jnp.float32),
        "col",
        scatter_dimension=0,
        tiled=True,
    )
    updated = panel_adj - 2.0 * reduced
    solved_adj = jnp.dot(
        updated, diag_inverse, precision=highest, preferred_element_type=jnp.float32
    )
    local_term = jnp.dot(solved_adj.T, panel, precision=highest, preferred_element_type=jnp.float32)
    corner = corner_adj - lax.psum(local_term, ("row", "col"))
    return (solved_adj, corner)


def solution(mesh):
    placed = (P("row", "col"), P(("row", "col"), None), P(("row", "col"), None), P(), P())
    return jax.shard_map(
        body, mesh=mesh, in_specs=placed, out_specs=(P(("row", "col"), None), P()), check_vma=False
    )
```

profile of v0, /device:TPU:1, one launch (start us, length us, event | category | flops | bytes accessed | tf_op | source)
XLA Modules:
  0.0 470.8 jit_solution(14945804477760813209)
XLA Ops:
  7.2 0.0 copy-start
  7.2 0.0 copy-start.3
  7.2 0.0 copy-start.4
  7.2 0.0 all-gather.2.cloned.1.call-start
  7.2 0.7 all-gather.2.cloned.1.call-update
  7.9 0.0 reduce-scatter.2.cloned.1.call-start
  8.0 0.0 copy-start.1
  8.0 132.7 %all-gather.2.cloned.1.call-done = f32[16384,256]{1,0:T(8,128)} async-done(((f32[64,256]{1,0:T(8,128)}), f32[16384,256]{1,0:T(8,128)}) %all-gather.2.cloned.1.call-update) | async-done | bytes 16777232 | tf_op jit(solution)/shard_map/all_gather | solution.py:13
  140.7 6.9 %convolution_bitcast_fusion = f32[1024,256]{1,0:T(8,128)} fusion(f32[1024,1024]{1,0:T(8,128)} %param.5, f32[16384,256]{1,0:T(8,128)} %all-gather.2.cloned.1.call-done, s32[]{:T(128)S(6)} %select_n.3), kind=kOutput, calls=%fused_computation | convolution fusion | flops 3221225472 | bytes 6291460 | tf_op jit(solution)/shard_map/dot_general | solution.py:16
  147.7 0.0 reduce-scatter.2.cloned.1.call-update
  147.7 0.0 all-reduce.2.cloned.1.call-start
  147.7 57.8 %reduce-scatter.2.cloned.1.call-done = f32[64,256]{1,0:T(8,128)} async-done(((f32[1024,256]{1,0:T(8,128)}), f32[64,256]{1,0:T(8,128)}) %reduce-scatter.2.cloned.1.call-update) | async-done | bytes 65552 | tf_op jit(solution)/shard_map/reduce_scatter | solution.py:15
  205.5 0.0 copy-done
  205.5 0.0 copy-done.4
  205.5 1.1 fusion.1
  206.6 0.0 copy-done.3
  206.6 0.0 copy-start.2
  206.6 1.1 fusion.7
  207.7 0.0 all-reduce.2.cloned.1.call-update
  207.8 254.8 %all-reduce.2.cloned.1.call-done = f32[256,256]{1,0:T(8,128)} async-done(((f32[256,256]{1,0:T(8,128)}), f32[256,256]{1,0:T(8,128)}) %all-reduce.2.cloned.1.call-update) | async-done | bytes 262160 | tf_op jit(solution)/shard_map/psum | solution.py:26
  462.5 0.0 copy-done.1
  462.6 1.7 sub.7
  464.2 0.0 copy-done.2
Async XLA Ops:
  7.2 198.3 %copy-start = (f32[256,256]{1,0:T(8,128)S(1)}, f32[256,256]{1,0:T(8,128)}, u32[]{:S(2)}) copy-start(f32[256,256]{1,0:T(8,128)} %param.8) | copy-start | bytes 786436
  7.2 199.4 %copy-start.3 = (f32[64,256]{1,0:T(8,128)S(1)}, f32[64,256]{1,0:T(8,128)}, u32[]{:S(2)}) copy-start(f32[64,256]{1,0:T(8,128)} %param.6) | copy-start | bytes 196612
  7.2 198.3 %copy-start.4 = (f32[64,256]{1,0:T(8,128)S(1)}, f32[64,256]{1,0:T(8,128)}, u32[]{:S(2)}) copy-start(f32[64,256]{1,0:T(8,128)} %param.7) | copy-start | bytes 196612
  7.2 133.5 %all-gather.2.cloned.1.call-start = ((), (), s32[]{:S(2)}) async-start(), calls=%async_computation.1 | async-start | bytes 16842752 | tf_op jit(solution)/shard_map/all_gather | solution.py:13
  7.9 197.6 %reduce-scatter.2.cloned.1.call-start = ((), (), s32[]{:S(2)}) async-start(), calls=%async_computation.2 | async-start | bytes 1114112 | tf_op jit(solution)/shard_map/reduce_scatter | solution.py:15
  8.0 454.6 %copy-start.1 = (f32[256,256]{1,0:T(8,128)S(1)}, f32[256,256]{1,0:T(8,128)}, u32[]{:S(2)}) copy-start(f32[256,256]{1,0:T(8,128)} %param.9) | copy-start | bytes 786436
  147.7 314.9 %all-reduce.2.cloned.1.call-start = ((), (), s32[]{:S(2)}) async-start(), calls=%async_computation.3 | async-start | bytes 524288 | tf_op jit(solution)/shard_map/psum | solution.py:26
  206.6 257.6 %copy-start.2 = (f32[64,256]{1,0:T(8,128)}, f32[64,256]{1,0:T(8,128)S(1)}, u32[]{:S(2)}) copy-start(f32[64,256]{1,0:T(8,128)S(1)} %fusion.1) | copy-start | bytes 196612
Sparse Core Ops, SparseCore 0:
  11.6 129.0 all-gather.1
  147.8 57.6 reduce-scatter.1
  212.4 250.0 all-reduce.1
where the time goes:
time: 472 us; the launch traced here: 471 us
  waiting for transfers between devices  446 us (94%)
  between operations  13.8 us (3%)
  matrix products  9.12 us (2%)
    psum x1, waiting for transfers between devices, body(): corner = corner_adj - lax.psum(local_term, ('row', 'col'))  255 us
    all_gather x1, waiting for transfers between devices, body(): whole = lax.all_gather(panel, ('row', 'col'), axis=0, tiled=True)  133 us
    reduce_scatter x1, waiting for transfers between devices, body(): lax.psum_scatter(jnp.dot(trail_adj, col_block, precision=highest, preferr...  57.8 us
  transfers between devices with their start and end apart: 3, of which 3 were waited for; matrix products, arithmetic and copies ran while one was open for 0% of the time, Pallas kernels for 0%

commit v1 on v0

v1 whole, which is shorter than its diff:
```python
import functools

import jax
import jax.numpy as jnp
from jax import lax
from jax.experimental import pallas as pl
from jax.experimental.pallas import tpu as pltpu
from jax.sharding import PartitionSpec as P

MESH = pl.DeviceIdType.MESH
F32 = jnp.float32
BF16 = jnp.bfloat16


def split(value):
    high = value.astype(BF16)
    return high, (value - high.astype(F32)).astype(BF16)


def dot3(a_high, a_low, b_high, b_low):
    dot = functools.partial(jnp.dot, preferred_element_type=F32)
    return dot(a_high, b_high) + (dot(a_high, b_low) + dot(a_low, b_high))


def kernel(
    t_hbm, p_hbm, a_hbm, d_hbm, c_hbm, solved_ref, corner_ref,
    t_raw, t_high, t_low, p_own, a_own, d_raw, c_raw, d_high, d_low,
    p_col, p_row, pt_high, pt_low, product,
    sibling, pair_sum, pair_in, m_own, m_in, m_sum, m_plane, md_own, md,
    local_sem, spread_send, col_recv, relay_send,
    row_send, row_fwd, row_recv, sib_send, sib_recv, pair_send, pair_recv,
    m_send, m_recv, z_send, z_recv, out_send, out_recv,
):
    row, col = lax.axis_index("row"), lax.axis_index("col")
    y, z_hi = row // 4, lax.rem(row, 4)
    z_lo, in_plane, core = col // 8, lax.rem(col, 8), lax.rem(col, 2)
    chip = col // 2
    z = z_hi * 2 + z_lo
    place = y * 8 + in_plane
    own_quarter, own_eighth = col // 4, lax.rem(col, 4)

    def in_plane_id(which):
        return ((which // 8) * 4 + z_hi, z_lo * 8 + lax.rem(which, 8))

    def z_id(which):
        return (y * 4 + which // 2, lax.rem(which, 2) * 8 + in_plane)

    slabs = [
        pltpu.make_async_copy(
            t_hbm.at[pl.ds(256 * i, 256)], t_raw.at[pl.ds(256 * i, 256)], local_sem.at[i]
        )
        for i in range(4)
    ]
    p_copy = pltpu.make_async_copy(p_hbm, p_own, local_sem.at[4])
    a_copy = pltpu.make_async_copy(a_hbm, a_own, local_sem.at[5])
    d_copy = pltpu.make_async_copy(d_hbm, d_raw, local_sem.at[6])
    c_copy = pltpu.make_async_copy(c_hbm, c_raw, local_sem.at[7])
    for copy in [p_copy, a_copy] + slabs + [d_copy, c_copy]:
        copy.start()

    barrier = pltpu.get_barrier_semaphore()

    def greet(device_id):
        pl.semaphore_signal(barrier, inc=1, device_id=device_id, device_id_type=MESH)

    diagonal = row == col
    for i in range(4):
        @pl.when(jnp.logical_not(jnp.logical_and(diagonal, own_eighth == i)))
        def _(i=i):
            greet((col, y * 4 + i))

    @pl.loop(1, 8)
    def _(step):
        greet(z_id(lax.rem(z + step, 8)))

    @pl.loop(1, 8)
    def _(step):
        greet((row, lax.rem(chip + step, 8) * 2 + core))

    @pl.loop(1, 32)
    def _(step):
        greet(in_plane_id(lax.rem(place + step, 32)))

    p_copy.wait()
    a_copy.wait()
    p_high, p_low = split(p_own[...])
    a_high, a_low = split(a_own[...])
    m_own[...] = dot3(p_high.T, p_low.T, a_high, a_low).reshape(32, 8, 256)
    p_row[col] = p_own[...]
    for i in range(4):
        slabs[i].wait()

        @pl.loop(0, 4)
        def _(j, i=i):
            rows = pl.ds(256 * i, 256)
            high, low = split(t_raw[rows, pl.ds(pl.multiple_of(256 * j, 256), 256)])
            t_high[j, rows] = high
            t_low[j, rows] = low

    d_copy.wait()
    high, low = split(d_raw[...])
    d_high[...] = high
    d_low[...] = low

    pl.semaphore_wait(barrier, 4 + 7 + 7 + 31 - diagonal.astype(jnp.int32))

    def spread(i):
        return pltpu.make_async_remote_copy(
            src_ref=p_own,
            dst_ref=p_col.at[own_quarter, pl.ds(pl.multiple_of(64 * own_eighth, 64), 64)],
            send_sem=spread_send.at[i],
            recv_sem=col_recv.at[own_quarter, own_eighth],
            device_id=(own_quarter * 4 + i, row),
            device_id_type=MESH,
        )

    def spread_self():
        return pltpu.make_async_copy(
            p_own,
            p_col.at[own_quarter, pl.ds(pl.multiple_of(64 * own_eighth, 64), 64)],
            col_recv.at[own_quarter, own_eighth],
        )

    for i in range(4):
        to_self = jnp.logical_and(diagonal, z_hi == i)

        @pl.when(to_self)
        def _():
            spread_self().start()

        @pl.when(jnp.logical_not(to_self))
        def _(i=i):
            spread(i).start()

    def relay(i, step):
        piece = p_col.at[y, pl.ds(64 * i, 64)]
        return pltpu.make_async_remote_copy(
            src_ref=piece,
            dst_ref=piece,
            send_sem=relay_send.at[i, step - 1],
            recv_sem=col_recv.at[y, i],
            device_id=(lax.rem(y + step, 4) * 4 + z_hi, col),
            device_id_type=MESH,
        )

    def arrived(quarter, i):
        piece = p_col.at[quarter, pl.ds(64 * i, 64)]
        pltpu.make_async_copy(p_own, piece, col_recv.at[quarter, i]).wait()

    for i in range(4):
        arrived(y, i)
        for step in (2, 1, 3):
            relay(i, step).start()

    def to_row(step):
        return pltpu.make_async_remote_copy(
            src_ref=p_own,
            dst_ref=p_row.at[col],
            send_sem=row_send.at[step],
            recv_sem=row_recv.at[col],
            device_id=(row, lax.rem(chip + step, 8) * 2 + core),
            device_id_type=MESH,
        )

    def to_sibling(step):
        block = p_row.at[lax.rem(chip + step, 8) * 2 + core]
        return pltpu.make_async_remote_copy(
            src_ref=block,
            dst_ref=block,
            send_sem=row_fwd.at[step],
            recv_sem=row_recv.at[lax.rem(chip + step, 8) * 2 + core],
            device_id=(row, chip * 2 + 1 - core),
            device_id_type=MESH,
        )

    @pl.loop(1, 8)
    def _(step):
        to_row(step).start()

    to_sibling(0).start()

    def add_quarter(quarter, first):
        high, low = split(p_col[quarter])

        @pl.loop(0, 4)
        def _(i):
            rows = pl.ds(pl.multiple_of(256 * i, 256), 256)
            term = dot3(t_high[quarter, rows], t_low[quarter, rows], high, low)
            place = pl.ds(2 * i, 2)
            term = term.reshape(2, 2, 64, 256)
            product[place] = term if first else product[place] + term

    add_quarter(y, True)

    @pl.loop(1, 8)
    def _(step):
        block = p_row.at[lax.rem(chip + step, 8) * 2 + core]
        pltpu.make_async_copy(p_own, block, row_recv.at[lax.rem(chip + step, 8) * 2 + core]).wait()
        to_sibling(step).start()

    for step in (1, 3):
        quarter = lax.rem(y + step, 4)
        for i in range(4):
            arrived(quarter, i)
        add_quarter(quarter, False)

    @pl.loop(0, 8)
    def _(step):
        which = step * 2 + 1 - core
        pltpu.make_async_copy(p_own, p_row.at[which], row_recv.at[which]).wait()

    for i in range(4):
        high, low = split(p_row[pl.ds(4 * i, 4)].reshape(256, 256))
        pt_high[:, pl.ds(256 * i, 256)] = high.T
        pt_low[:, pl.ds(256 * i, 256)] = low.T

    quarter = lax.rem(y + 2, 4)
    for i in range(4):
        arrived(quarter, i)
    add_quarter(quarter, False)

    total = jnp.zeros((256, 256), F32)
    for i in range(4):
        high, low = split(product[pl.ds(2 * i, 2)].reshape(256, 256))
        total += dot3(pt_high[:, pl.ds(256 * i, 256)], pt_low[:, pl.ds(256 * i, 256)], high, low)
    m_own[...] = m_own[...] - 2.0 * total.reshape(32, 8, 256)
    m_in[place] = m_own[place]

    def to_plane(step):
        which = lax.rem(place + step, 32)
        return pltpu.make_async_remote_copy(
            src_ref=m_own.at[which],
            dst_ref=m_in.at[place],
            send_sem=m_send.at[step],
            recv_sem=m_recv.at[place],
            device_id=in_plane_id(which),
            device_id_type=MESH,
        )

    @pl.loop(1, 32)
    def _(step):
        to_plane(step).start()

    to_pair = pltpu.make_async_remote_copy(
        src_ref=product.at[:, 1 - core],
        dst_ref=sibling,
        send_sem=sib_send,
        recv_sem=sib_recv,
        device_id=(row, chip * 2 + 1 - core),
        device_id_type=MESH,
    )
    to_pair.start()
    to_pair.wait_recv()
    for i in range(8):
        pair_sum[i] = product[i, core] + sibling[i]

    def to_chip(step):
        which = lax.rem(chip + step, 8)
        return pltpu.make_async_remote_copy(
            src_ref=pair_sum.at[which],
            dst_ref=pair_in.at[chip],
            send_sem=pair_send.at[step],
            recv_sem=pair_recv.at[chip],
            device_id=(row, which * 2 + core),
            device_id_type=MESH,
        )

    @pl.loop(1, 8)
    def _(step):
        to_chip(step).start()

    @pl.loop(1, 32)
    def _(step):
        which = lax.rem(place + step, 32)
        pltpu.make_async_copy(md_own, m_in.at[which], m_recv.at[which]).wait()

    total = m_in[0]
    for i in range(1, 32):
        total += m_in[i]
    m_sum[...] = total
    m_plane[z] = total

    def to_z(step):
        return pltpu.make_async_remote_copy(
            src_ref=m_sum,
            dst_ref=m_plane.at[z],
            send_sem=z_send.at[step],
            recv_sem=z_recv.at[z],
            device_id=z_id(lax.rem(z + step, 8)),
            device_id_type=MESH,
        )

    @pl.loop(1, 8)
    def _(step):
        to_z(step).start()

    @pl.loop(1, 8)
    def _(step):
        which = lax.rem(z + step, 8)
        pltpu.make_async_copy(md_own, m_plane.at[which], z_recv.at[which]).wait()

    total = m_plane[0]
    for i in range(1, 8):
        total += m_plane[i]
    high, low = split(jnp.concatenate([total, total], axis=0))
    total = dot3(high, low, d_high[...], d_low[...])[0:8]
    md_own[...] = total
    md[place] = total

    def to_all(step):
        return pltpu.make_async_remote_copy(
            src_ref=md_own,
            dst_ref=md.at[place],
            send_sem=out_send.at[step],
            recv_sem=out_recv.at[place],
            device_id=in_plane_id(lax.rem(place + step, 32)),
            device_id_type=MESH,
        )

    @pl.loop(1, 32)
    def _(step):
        to_all(step).start()

    @pl.loop(1, 8)
    def _(step):
        which = lax.rem(chip + step, 8)
        pltpu.make_async_copy(p_own, pair_in.at[which], pair_recv.at[which]).wait()

    reduced = pair_sum[chip]
    for step in range(1, 8):
        reduced += pair_in[lax.rem(chip + step, 8)]
    high, low = split(a_own[...] - 2.0 * reduced)
    solved_ref[...] = dot3(high, low, d_high[...], d_low[...])
    c_copy.wait()

    for i in range(4):
        @pl.when(jnp.logical_not(jnp.logical_and(diagonal, z_hi == i)))
        def _(i=i):
            spread(i).wait_send()

        for step in (1, 2, 3):
            relay(i, step).wait_send()
    to_sibling(0).wait_send()
    to_pair.wait_send()

    @pl.loop(1, 8)
    def _(step):
        to_row(step).wait_send()
        to_sibling(step).wait_send()
        to_chip(step).wait_send()
        to_z(step).wait_send()

    @pl.loop(1, 32)
    def _(step):
        to_plane(step).wait_send()

    @pl.loop(1, 32)
    def _(step):
        which = lax.rem(place + step, 32)
        pltpu.make_async_copy(md_own, md.at[which], out_recv.at[which]).wait()

    corner_ref[...] = c_raw[...] - md[...].reshape(256, 256).T

    @pl.loop(1, 32)
    def _(step):
        to_all(step).wait_send()


def body(trail_adj, panel, panel_adj, diag_inverse, corner_adj):
    hbm = pl.BlockSpec(memory_space=pl.ANY)
    vmem = pl.BlockSpec(memory_space=pltpu.VMEM)
    dma = pltpu.SemaphoreType.DMA
    return pl.pallas_call(
        kernel,
        out_shape=(
            jax.ShapeDtypeStruct((64, 256), F32),
            jax.ShapeDtypeStruct((256, 256), F32),
        ),
        in_specs=[hbm] * 5,
        out_specs=(vmem, vmem),
        scratch_shapes=[
            pltpu.VMEM((1024, 1024), F32),
            pltpu.VMEM((4, 1024, 256), BF16),
            pltpu.VMEM((4, 1024, 256), BF16),
            pltpu.VMEM((64, 256), F32),
            pltpu.VMEM((64, 256), F32),
            pltpu.VMEM((256, 256), F32),
            pltpu.VMEM((256, 256), F32),
            pltpu.VMEM((256, 256), BF16),
            pltpu.VMEM((256, 256), BF16),
            pltpu.VMEM((4, 256, 256), F32),
            pltpu.VMEM((16, 64, 256), F32),
            pltpu.VMEM((256, 1024), BF16),
            pltpu.VMEM((256, 1024), BF16),
            pltpu.VMEM((8, 2, 64, 256), F32),
            pltpu.VMEM((8, 64, 256), F32),
            pltpu.VMEM((8, 64, 256), F32),
            pltpu.VMEM((8, 64, 256), F32),
            pltpu.VMEM((32, 8, 256), F32),
            pltpu.VMEM((32, 8, 256), F32),
            pltpu.VMEM((8, 256), F32),
            pltpu.VMEM((8, 8, 256), F32),
            pltpu.VMEM((8, 256), F32),
            pltpu.VMEM((32, 8, 256), F32),
            dma((8,)),
            dma((4,)),
            dma((4, 4)),
            dma((4, 3)),
            dma((8,)),
            dma((8,)),
            dma((16,)),
            dma(()),
            dma(()),
            dma((8,)),
            dma((8,)),
            dma((32,)),
            dma((32,)),
            dma((8,)),
            dma((8,)),
            dma((32,)),
            dma((32,)),
        ],
        compiler_params=pltpu.CompilerParams(
            collective_id=0, has_side_effects=True, vmem_limit_bytes=40 * 1024 * 1024
        ),
        name="adjoint_panel",
    )(trail_adj, panel, panel_adj, diag_inverse, corner_adj)


def solution(mesh):
    placed = (P("row", "col"), P(("row", "col"), None), P(("row", "col"), None), P(), P())
    return jax.shard_map(
        body, mesh=mesh, in_specs=placed, out_specs=(P(("row", "col"), None), P()), check_vma=False
    )
```

time: 472 us -> 74 us (0.16)
  waiting for transfers between devices: 446 us -> 0 us
  Pallas kernels: 0 us -> 66 us
  between operations: 13.8 us -> 0.65 us
  matrix products: 9.12 us -> 0 us
  local copies, waits for them, and re-layouts: 0.03 us -> 7.09 us
    psum x1 -> x0, waiting for transfers between devices: 255 us -> none  [body(): corner = corner_adj - lax.psum(local_term, ('row', 'col'))]
    all_gather x1 -> x0, waiting for transfers between devices: 133 us -> none  [body(): whole = lax.all_gather(panel, ('row', 'col'), axis=0, tiled=True)]
    pallas_call x0 -> x1, Pallas kernels: none -> 66 us  [body(): pl.pallas_call(kernel, out_shape=(jax.ShapeDtypeStruct((64, 256), F32), j...]
    reduce_scatter x1 -> x0, waiting for transfers between devices: 57.8 us -> none  [body(): lax.psum_scatter(jnp.dot(trail_adj, col_block, precision=highest, preferr...]
    dot_general x3 -> x0, matrix products: 9.12 us -> none  [the longest x1 6.93 us: body(): jnp.dot(trail_adj, col_block, precision=highest, preferred_element_type=j...]
    unnamed x10 -> x12, local copies, waits for them, and re-layouts: 0.03 us -> 7.09 us
  transfers between devices with their start and end apart: 3 -> 0, of which waited for: 3 -> 0; matrix products, arithmetic and copies ran while one was open for 0% -> 0% of each run, Pallas kernels for 0% -> 0%
where the time goes in v1:
time: 74 us; the launch traced here: 73.8 us
  Pallas kernels  66 us (89%)
  local copies, waits for them, and re-layouts  7.09 us (10%)
    pallas_call x1, Pallas kernels, body(): pl.pallas_call(kernel, out_shape=(jax.ShapeDtypeStruct((64, 256), F32), j...  66 us
    unnamed x12, local copies, waits for them, and re-layouts  7.09 us

profile of v1, /device:TPU:1, one launch (start us, length us, event | category | flops | bytes accessed | tf_op | source)
XLA Modules:
  0.0 73.8 jit_solution(8310975311664427207)
XLA Ops:
  0.6 0.0 copy-start
  0.6 2.2 %copy-done = f32[1024,1024]{1,0:T(8,128)S(1)} copy-done((f32[1024,1024]{1,0:T(8,128)S(1)}, f32[1024,1024]{1,0:T(8,128)}, u32[]{:S(2)}) %copy-start) | copy-done | bytes 4194328
  2.8 0.0 copy-start.1
  2.8 0.9 %copy-done.1 = f32[256,256]{1,0:T(8,128)S(1)} copy-done((f32[256,256]{1,0:T(8,128)S(1)}, f32[256,256]{1,0:T(8,128)}, u32[]{:S(2)}) %copy-start.1) | copy-done | bytes 262168
  3.8 0.0 copy-start.2
  3.8 0.9 %copy-done.2 = f32[256,256]{1,0:T(8,128)S(1)} copy-done((f32[256,256]{1,0:T(8,128)S(1)}, f32[256,256]{1,0:T(8,128)}, u32[]{:S(2)}) %copy-start.2) | copy-done | bytes 262168
  4.7 0.0 copy-start.3
  4.7 0.8 %copy-done.3 = f32[64,256]{1,0:T(8,128)S(1)} copy-done((f32[64,256]{1,0:T(8,128)S(1)}, f32[64,256]{1,0:T(8,128)}, u32[]{:S(2)}) %copy-start.3) | copy-done | bytes 65560
  5.6 0.0 copy-start.4
  5.6 0.8 %copy-done.4 = f32[64,256]{1,0:T(8,128)S(1)} copy-done((f32[64,256]{1,0:T(8,128)S(1)}, f32[64,256]{1,0:T(8,128)}, u32[]{:S(2)}) %copy-start.4) | copy-done | bytes 65560
  6.4 66.0 %adjoint_panel.1 = (f32[64,256]{1,0:T(8,128)S(1)}, f32[256,256]{1,0:T(8,128)S(1)}) custom-call(f32[1024,1024]{1,0:T(8,128)S(1)} %copy-done, f32[64,256]{1,0:T(8,128)S(1)} %copy-done.3, f32[64,256]{1,0:T(8,128)S(1)} %copy-done.4, f32[256,256]{1,0:T(8,128)S(1)} %copy-done.1, f32[256,256]{1,0:T(8,128)S(1)} %copy-done.2), custom_call_target="tpu_custom_call" | custom-call | tf_op jit(solution)/shard_map/adjoint_panel/pallas_call | solution.py:373
  72.4 0.6 copy.9
  73.1 0.7 copy.10
Async XLA Ops:
  0.6 2.2 %copy-start = (f32[1024,1024]{1,0:T(8,128)S(1)}, f32[1024,1024]{1,0:T(8,128)}, u32[]{:S(2)}) copy-start(f32[1024,1024]{1,0:T(8,128)} %t_hbm.1) | copy-start | bytes 12582916
  2.8 0.9 %copy-start.1 = (f32[256,256]{1,0:T(8,128)S(1)}, f32[256,256]{1,0:T(8,128)}, u32[]{:S(2)}) copy-start(f32[256,256]{1,0:T(8,128)} %d_hbm.1) | copy-start | bytes 786436
  3.8 0.9 %copy-start.2 = (f32[256,256]{1,0:T(8,128)S(1)}, f32[256,256]{1,0:T(8,128)}, u32[]{:S(2)}) copy-start(f32[256,256]{1,0:T(8,128)} %c_hbm.1) | copy-start | bytes 786436
  4.7 0.8 %copy-start.3 = (f32[64,256]{1,0:T(8,128)S(1)}, f32[64,256]{1,0:T(8,128)}, u32[]{:S(2)}) copy-start(f32[64,256]{1,0:T(8,128)} %p_hbm.1) | copy-start | bytes 196612
  5.6 0.8 %copy-start.4 = (f32[64,256]{1,0:T(8,128)S(1)}, f32[64,256]{1,0:T(8,128)}, u32[]{:S(2)}) copy-start(f32[64,256]{1,0:T(8,128)} %a_hbm.1) | copy-start | bytes 196612

commit v2 on v1

--- a/solution.py
+++ b/solution.py
@@ -27,7 +27,7 @@
     t_raw, t_high, t_low, p_own, a_own, d_raw, c_raw, d_high, d_low,
     p_col, p_row, pt_high, pt_low, product,
     sibling, pair_sum, pair_in, m_own, m_in, m_sum, m_plane, md_own, md,
-    local_sem, spread_send, col_recv, relay_send,
+    local_sem, spread_send, col_recv, turn_send, relay_send,
     row_send, row_fwd, row_recv, sib_send, sib_recv, pair_send, pair_recv,
     m_send, m_recv, z_send, z_recv, out_send, out_recv,
 ):
@@ -37,7 +37,8 @@
     chip = col // 2
     z = z_hi * 2 + z_lo
     place = y * 8 + in_plane
-    own_quarter, own_eighth = col // 4, lax.rem(col, 4)
+    own_quarter, own_piece = col // 4, lax.rem(col, 4)
+    odd = lax.rem(z_hi, 2)
 
     def in_plane_id(which):
         return ((which // 8) * 4 + z_hi, z_lo * 8 + lax.rem(which, 8))
@@ -64,10 +65,10 @@
         pl.semaphore_signal(barrier, inc=1, device_id=device_id, device_id_type=MESH)
 
     diagonal = row == col
-    for i in range(4):
-        @pl.when(jnp.logical_not(jnp.logical_and(diagonal, own_eighth == i)))
+    for i in range(2):
+        @pl.when(jnp.logical_not(jnp.logical_and(diagonal, z_hi // 2 == i)))
         def _(i=i):
-            greet((col, y * 4 + i))
+            greet((col, y * 4 + odd + 2 * i))
 
     @pl.loop(1, 8)
     def _(step):
@@ -102,27 +103,27 @@
     d_high[...] = high
     d_low[...] = low
 
-    pl.semaphore_wait(barrier, 4 + 7 + 7 + 31 - diagonal.astype(jnp.int32))
+    pl.semaphore_wait(barrier, 2 + 7 + 7 + 31 - diagonal.astype(jnp.int32))
 
     def spread(i):
         return pltpu.make_async_remote_copy(
             src_ref=p_own,
-            dst_ref=p_col.at[own_quarter, pl.ds(pl.multiple_of(64 * own_eighth, 64), 64)],
+            dst_ref=p_col.at[own_quarter, pl.ds(pl.multiple_of(64 * own_piece, 64), 64)],
             send_sem=spread_send.at[i],
-            recv_sem=col_recv.at[own_quarter, own_eighth],
-            device_id=(own_quarter * 4 + i, row),
+            recv_sem=col_recv.at[own_quarter, own_piece],
+            device_id=(own_quarter * 4 + lax.rem(own_piece, 2) + 2 * i, row),
             device_id_type=MESH,
         )
 
     def spread_self():
         return pltpu.make_async_copy(
             p_own,
-            p_col.at[own_quarter, pl.ds(pl.multiple_of(64 * own_eighth, 64), 64)],
-            col_recv.at[own_quarter, own_eighth],
-        )
-
-    for i in range(4):
-        to_self = jnp.logical_and(diagonal, z_hi == i)
+            p_col.at[own_quarter, pl.ds(pl.multiple_of(64 * own_piece, 64), 64)],
+            col_recv.at[own_quarter, own_piece],
+        )
+
+    for i in range(2):
+        to_self = jnp.logical_and(diagonal, z_hi // 2 == i)
 
         @pl.when(to_self)
         def _():
@@ -132,23 +133,40 @@
         def _(i=i):
             spread(i).start()
 
+    pieces = (odd, odd + 2, 1 - odd, 3 - odd)
+
+    def turn(i):
+        which = pieces[i]
+        piece = p_col.at[y, pl.ds(pl.multiple_of(64 * which, 64), 64)]
+        return pltpu.make_async_remote_copy(
+            src_ref=piece,
+            dst_ref=piece,
+            send_sem=turn_send.at[i],
+            recv_sem=col_recv.at[y, which],
+            device_id=(y * 4 + lax.rem(z_hi + 1 + 2 * i, 4), col),
+            device_id_type=MESH,
+        )
+
     def relay(i, step):
-        piece = p_col.at[y, pl.ds(64 * i, 64)]
+        which = pieces[i]
+        piece = p_col.at[y, pl.ds(pl.multiple_of(64 * which, 64), 64)]
         return pltpu.make_async_remote_copy(
             src_ref=piece,
             dst_ref=piece,
             send_sem=relay_send.at[i, step - 1],
-            recv_sem=col_recv.at[y, i],
+            recv_sem=col_recv.at[y, which],
             device_id=(lax.rem(y + step, 4) * 4 + z_hi, col),
             device_id_type=MESH,
         )
 
     def arrived(quarter, i):
-        piece = p_col.at[quarter, pl.ds(64 * i, 64)]
+        piece = p_col.at[quarter, pl.ds(pl.multiple_of(64 * i, 64), 64)]
         pltpu.make_async_copy(p_own, piece, col_recv.at[quarter, i]).wait()
 
     for i in range(4):
-        arrived(y, i)
+        arrived(y, pieces[i])
+        if i < 2:
+            turn(i).start()
         for step in (2, 1, 3):
             relay(i, step).start()
 
@@ -265,10 +283,6 @@
             device_id_type=MESH,
         )
 
-    @pl.loop(1, 8)
-    def _(step):
-        to_chip(step).start()
-
     @pl.loop(1, 32)
     def _(step):
         which = lax.rem(place + step, 32)
@@ -293,6 +307,10 @@
     @pl.loop(1, 8)
     def _(step):
         to_z(step).start()
+
+    @pl.loop(1, 8)
+    def _(step):
+        to_chip(step).start()
 
     @pl.loop(1, 8)
     def _(step):
@@ -333,11 +351,14 @@
     solved_ref[...] = dot3(high, low, d_high[...], d_low[...])
     c_copy.wait()
 
-    for i in range(4):
-        @pl.when(jnp.logical_not(jnp.logical_and(diagonal, z_hi == i)))
+    for i in range(2):
+        @pl.when(jnp.logical_not(jnp.logical_and(diagonal, z_hi // 2 == i)))
         def _(i=i):
             spread(i).wait_send()
 
+        turn(i).wait_send()
+
+    for i in range(4):
         for step in (1, 2, 3):
             relay(i, step).wait_send()
     to_sibling(0).wait_send()
@@ -405,6 +426,7 @@
             dma((8,)),
             dma((4,)),
             dma((4, 4)),
+            dma((2,)),
             dma((4, 3)),
             dma((8,)),
             dma((8,)),
@@ -421,7 +443,7 @@
             dma((32,)),
         ],
         compiler_params=pltpu.CompilerParams(
-            collective_id=0, has_side_effects=True, vmem_limit_bytes=40 * 1024 * 1024
+            collective_id=0, has_side_effects=True, vmem_limit_bytes=60 * 1024 * 1024
         ),
         name="adjoint_panel",
     )(trail_adj, panel, panel_adj, diag_inverse, corner_adj)

time: 74 us -> 63.4 us (0.86)
  Pallas kernels: 66 us -> 59.4 us
  local copies, waits for them, and re-layouts: 7.09 us -> 3.14 us
    pallas_call x1, Pallas kernels: 66 us -> 59.4 us  [body(): pl.pallas_call(kernel, out_shape=(jax.ShapeDtypeStruct((64, 256), F32), j...]
    unnamed x12 -> x2, local copies, waits for them, and re-layouts: 7.09 us -> 3.14 us
where the time goes in v2:
time: 63.4 us; the launch traced here: 63.2 us
  Pallas kernels  59.4 us (94%)
  local copies, waits for them, and re-layouts  3.14 us (5%)
  between operations  0.64 us (1%)
    pallas_call x1, Pallas kernels, body(): pl.pallas_call(kernel, out_shape=(jax.ShapeDtypeStruct((64, 256), F32), j...  59.4 us
    unnamed x2, local copies, waits for them, and re-layouts  3.14 us

profile of v2, /device:TPU:1, one launch (start us, length us, event | category | flops | bytes accessed | tf_op | source)
XLA Modules:
  0.0 63.2 jit_solution(8243039047417212840)
XLA Ops:
  0.6 59.4 %adjoint_panel.1 = (f32[64,256]{1,0:T(8,128)}, f32[256,256]{1,0:T(8,128)}) custom-call(f32[1024,1024]{1,0:T(8,128)} %t_hbm.1, f32[64,256]{1,0:T(8,128)} %p_hbm.1, f32[64,256]{1,0:T(8,128)} %a_hbm.1, f32[256,256]{1,0:T(8,128)} %d_hbm.1, f32[256,256]{1,0:T(8,128)} %c_hbm.1), custom_call_target="tpu_custom_call" | custom-call | tf_op jit(solution)/shard_map/adjoint_panel/pallas_call | solution.py:394
  60.1 1.5 %copy.9 = f32[64,256]{1,0:T(8,128)} copy(f32[64,256]{1,0:T(8,128)} %get-tuple-element.4) | data formatting | bytes 131072
  61.5 1.7 %copy.10 = f32[256,256]{1,0:T(8,128)} copy(f32[256,256]{1,0:T(8,128)} %get-tuple-element.5) | data formatting | bytes 524288

commit v3 on v2

--- a/solution.py
+++ b/solution.py
@@ -25,7 +25,7 @@
 def kernel(
     t_hbm, p_hbm, a_hbm, d_hbm, c_hbm, solved_ref, corner_ref,
     t_raw, t_high, t_low, p_own, a_own, d_raw, c_raw, d_high, d_low,
-    p_col, p_row, pt_high, pt_low, product,
+    p_col, p_row, pt_high, pt_low, pt_t_high, pt_t_low, p_col_high, p_col_low, product,
     sibling, pair_sum, pair_in, m_own, m_in, m_sum, m_plane, md_own, md,
     local_sem, spread_send, col_recv, turn_send, relay_send,
     row_send, row_fwd, row_recv, sib_send, sib_recv, pair_send, pair_recv,
@@ -74,9 +74,9 @@
     def _(step):
         greet(z_id(lax.rem(z + step, 8)))
 
-    @pl.loop(1, 8)
-    def _(step):
-        greet((row, lax.rem(chip + step, 8) * 2 + core))
+    @pl.loop(1, 4)
+    def _(step):
+        greet((row, (1 - z_lo) * 8 + lax.rem(in_plane + 2 * step, 8)))
 
     @pl.loop(1, 32)
     def _(step):
@@ -103,7 +103,7 @@
     d_high[...] = high
     d_low[...] = low
 
-    pl.semaphore_wait(barrier, 2 + 7 + 7 + 31 - diagonal.astype(jnp.int32))
+    pl.semaphore_wait(barrier, 2 + 7 + 3 + 31 - diagonal.astype(jnp.int32))
 
     def spread(i):
         return pltpu.make_async_remote_copy(
@@ -163,84 +163,86 @@
         piece = p_col.at[quarter, pl.ds(pl.multiple_of(64 * i, 64), 64)]
         pltpu.make_async_copy(p_own, piece, col_recv.at[quarter, i]).wait()
 
+    def to_partner():
+        return pltpu.make_async_remote_copy(
+            src_ref=p_own,
+            dst_ref=p_row.at[col],
+            send_sem=row_send.at[0],
+            recv_sem=row_recv.at[col],
+            device_id=(row, (1 - z_lo) * 8 + in_plane),
+            device_id_type=MESH,
+        )
+
+    def to_row(half, step):
+        which = lax.rem(z_lo + half, 2) * 8 + in_plane
+        block = p_row.at[which]
+        return pltpu.make_async_remote_copy(
+            src_ref=block,
+            dst_ref=block,
+            send_sem=row_send.at[half * 4 + step],
+            recv_sem=row_recv.at[which],
+            device_id=(row, z_lo * 8 + lax.rem(in_plane + 2 * step, 8)),
+            device_id_type=MESH,
+        )
+
+    def to_sibling(step):
+        which = lax.rem(chip + step, 8) * 2 + core
+        block = p_row.at[which]
+        return pltpu.make_async_remote_copy(
+            src_ref=block,
+            dst_ref=block,
+            send_sem=row_fwd.at[step],
+            recv_sem=row_recv.at[which],
+            device_id=(row, chip * 2 + 1 - core),
+            device_id_type=MESH,
+        )
+
+    def row_arrived(which):
+        pltpu.make_async_copy(p_own, p_row.at[which], row_recv.at[which]).wait()
+
+    to_partner().start()
+    to_sibling(0).start()
     for i in range(4):
         arrived(y, pieces[i])
         if i < 2:
             turn(i).start()
         for step in (2, 1, 3):
             relay(i, step).start()
-
-    def to_row(step):
-        return pltpu.make_async_remote_copy(
-            src_ref=p_own,
-            dst_ref=p_row.at[col],
-            send_sem=row_send.at[step],
-            recv_sem=row_recv.at[col],
-            device_id=(row, lax.rem(chip + step, 8) * 2 + core),
-            device_id_type=MESH,
-        )
-
-    def to_sibling(step):
-        block = p_row.at[lax.rem(chip + step, 8) * 2 + core]
-        return pltpu.make_async_remote_copy(
-            src_ref=block,
-            dst_ref=block,
-            send_sem=row_fwd.at[step],
-            recv_sem=row_recv.at[lax.rem(chip + step, 8) * 2 + core],
-            device_id=(row, chip * 2 + 1 - core),
-            device_id_type=MESH,
-        )
-
-    @pl.loop(1, 8)
-    def _(step):
-        to_row(step).start()
-
-    to_sibling(0).start()
-
-    def add_quarter(quarter, first):
-        high, low = split(p_col[quarter])
-
-        @pl.loop(0, 4)
-        def _(i):
-            rows = pl.ds(pl.multiple_of(256 * i, 256), 256)
-            term = dot3(t_high[quarter, rows], t_low[quarter, rows], high, low)
-            place = pl.ds(2 * i, 2)
-            term = term.reshape(2, 2, 64, 256)
-            product[place] = term if first else product[place] + term
-
-    add_quarter(y, True)
-
-    @pl.loop(1, 8)
-    def _(step):
-        block = p_row.at[lax.rem(chip + step, 8) * 2 + core]
-        pltpu.make_async_copy(p_own, block, row_recv.at[lax.rem(chip + step, 8) * 2 + core]).wait()
+        if i == 1:
+            for step in (2, 1, 3):
+                to_row(0, step).start()
+            row_arrived((1 - z_lo) * 8 + in_plane)
+            for step in (2, 1, 3):
+                to_row(1, step).start()
+            to_sibling(4).start()
+
+    for step in (1, 2, 3, 5, 6, 7):
+        row_arrived(lax.rem(chip + step, 8) * 2 + core)
         to_sibling(step).start()
 
-    for step in (1, 3):
-        quarter = lax.rem(y + step, 4)
-        for i in range(4):
-            arrived(quarter, i)
-        add_quarter(quarter, False)
-
-    @pl.loop(0, 8)
-    def _(step):
-        which = step * 2 + 1 - core
-        pltpu.make_async_copy(p_own, p_row.at[which], row_recv.at[which]).wait()
-
     for i in range(4):
+        for step in (0, 1):
+            row_arrived(4 * i + 2 * step + 1 - core)
         high, low = split(p_row[pl.ds(4 * i, 4)].reshape(256, 256))
         pt_high[:, pl.ds(256 * i, 256)] = high.T
         pt_low[:, pl.ds(256 * i, 256)] = low.T
 
-    quarter = lax.rem(y + 2, 4)
-    for i in range(4):
-        arrived(quarter, i)
-    add_quarter(quarter, False)
+    @pl.loop(0, 4)
+    def _(j):
+        high, low = split(dot3(pt_high[...], pt_low[...], t_high[j], t_low[j]))
+        pt_t_high[j] = high
+        pt_t_low[j] = low
 
     total = jnp.zeros((256, 256), F32)
-    for i in range(4):
-        high, low = split(product[pl.ds(2 * i, 2)].reshape(256, 256))
-        total += dot3(pt_high[:, pl.ds(256 * i, 256)], pt_low[:, pl.ds(256 * i, 256)], high, low)
+    for step in (0, 1, 3, 2):
+        quarter = lax.rem(y + step, 4)
+        if step:
+            for i in range(4):
+                arrived(quarter, i)
+        high, low = split(p_col[quarter])
+        p_col_high[quarter] = high
+        p_col_low[quarter] = low
+        total += dot3(pt_t_high[quarter], pt_t_low[quarter], high, low)
     m_own[...] = m_own[...] - 2.0 * total.reshape(32, 8, 256)
     m_in[place] = m_own[place]
 
@@ -258,6 +260,14 @@
     @pl.loop(1, 32)
     def _(step):
         to_plane(step).start()
+
+    @pl.loop(0, 4)
+    def _(i):
+        rows = pl.ds(pl.multiple_of(256 * i, 256), 256)
+        total = jnp.zeros((256, 256), F32)
+        for j in range(4):
+            total += dot3(t_high[j, rows], t_low[j, rows], p_col_high[j], p_col_low[j])
+        product[pl.ds(2 * i, 2)] = total.reshape(2, 2, 64, 256)
 
     to_pair = pltpu.make_async_remote_copy(
         src_ref=product.at[:, 1 - core],
@@ -362,11 +372,14 @@
         for step in (1, 2, 3):
             relay(i, step).wait_send()
     to_sibling(0).wait_send()
+    to_partner().wait_send()
+    for step in (1, 2, 3):
+        to_row(0, step).wait_send()
+        to_row(1, step).wait_send()
     to_pair.wait_send()
 
     @pl.loop(1, 8)
     def _(step):
-        to_row(step).wait_send()
         to_sibling(step).wait_send()
         to_chip(step).wait_send()
         to_z(step).wait_send()
@@ -374,6 +387,7 @@
     @pl.loop(1, 32)
     def _(step):
         to_plane(step).wait_send()
+        to_all(step).wait_send()
 
     @pl.loop(1, 32)
     def _(step):
@@ -382,13 +396,9 @@
 
     corner_ref[...] = c_raw[...] - md[...].reshape(256, 256).T
 
-    @pl.loop(1, 32)
-    def _(step):
-        to_all(step).wait_send()
-
-
-def body(trail_adj, panel, panel_adj, diag_inverse, corner_adj):
-    hbm = pl.BlockSpec(memory_space=pl.ANY)
+
+def body(*arrays):
+    hbm = pl.BlockSpec(memory_space=pltpu.HBM)
     vmem = pl.BlockSpec(memory_space=pltpu.VMEM)
     dma = pltpu.SemaphoreType.DMA
     return pl.pallas_call(
@@ -413,6 +423,10 @@
             pltpu.VMEM((16, 64, 256), F32),
             pltpu.VMEM((256, 1024), BF16),
             pltpu.VMEM((256, 1024), BF16),
+            pltpu.VMEM((4, 256, 256), BF16),
+            pltpu.VMEM((4, 256, 256), BF16),
+            pltpu.VMEM((4, 256, 256), BF16),
+            pltpu.VMEM((4, 256, 256), BF16),
             pltpu.VMEM((8, 2, 64, 256), F32),
             pltpu.VMEM((8, 64, 256), F32),
             pltpu.VMEM((8, 64, 256), F32),
@@ -443,10 +457,10 @@
             dma((32,)),
         ],
         compiler_params=pltpu.CompilerParams(
-            collective_id=0, has_side_effects=True, vmem_limit_bytes=60 * 1024 * 1024
+            collective_id=0, has_side_effects=True, vmem_limit_bytes=32 * 1024 * 1024
         ),
         name="adjoint_panel",
-    )(trail_adj, panel, panel_adj, diag_inverse, corner_adj)
+    )(*(pltpu.with_memory_space_constraint(x, pltpu.HBM) for x in arrays))
 
 
 def solution(mesh):

time: 63.4 us -> 57.1 us (0.901)
  Pallas kernels: 59.4 us -> 55.1 us
  local copies, waits for them, and re-layouts: 3.14 us -> 1.33 us
    pallas_call x1, Pallas kernels: 59.4 us -> 55.1 us  [body(): pl.pallas_call(kernel, out_shape=(jax.ShapeDtypeStruct((64, 256), F32), j...]
    unnamed x2, local copies, waits for them, and re-layouts: 3.14 us -> 1.33 us
where the time goes in v3:
time: 57.1 us; the launch traced here: 57 us
  Pallas kernels  55.1 us (96%)
  local copies, waits for them, and re-layouts  1.33 us (2%)
  between operations  0.64 us (1%)
    pallas_call x1, Pallas kernels, body(): pl.pallas_call(kernel, out_shape=(jax.ShapeDtypeStruct((64, 256), F32), j...  55.1 us
    unnamed x2, local copies, waits for them, and re-layouts  1.33 us

profile of v3, /device:TPU:1, one launch (start us, length us, event | category | flops | bytes accessed | tf_op | source)
XLA Modules:
  0.0 57.0 jit_solution(16421341683965779157)
XLA Ops:
  0.6 55.1 %adjoint_panel.1 = (f32[64,256]{1,0:T(8,128)S(1)}, f32[256,256]{1,0:T(8,128)S(1)}) custom-call(f32[1024,1024]{1,0:T(8,128)} %t_hbm.1, f32[64,256]{1,0:T(8,128)} %p_hbm.1, f32[64,256]{1,0:T(8,128)} %a_hbm.1, f32[256,256]{1,0:T(8,128)} %d_hbm.1, f32[256,256]{1,0:T(8,128)} %c_hbm.1), custom_call_target="tpu_custom_call" | custom-call | tf_op jit(solution)/shard_map/adjoint_panel/pallas_call | solution.py:404
  55.7 0.6 %copy.9 = f32[64,256]{1,0:T(8,128)} copy(f32[64,256]{1,0:T(8,128)S(1)} %get-tuple-element.4) | data formatting | bytes 131072
  56.3 0.7 %copy.10 = f32[256,256]{1,0:T(8,128)} copy(f32[256,256]{1,0:T(8,128)S(1)} %get-tuple-element.5) | data formatting | bytes 524288

commit v4 on v3

--- a/solution.py
+++ b/solution.py
@@ -27,7 +27,7 @@
     t_raw, t_high, t_low, p_own, a_own, d_raw, c_raw, d_high, d_low,
     p_col, p_row, pt_high, pt_low, pt_t_high, pt_t_low, p_col_high, p_col_low, product,
     sibling, pair_sum, pair_in, m_own, m_in, m_sum, m_plane, md_own, md,
-    local_sem, spread_send, col_recv, turn_send, relay_send,
+    local_sem, spread_send, col_recv, z_relay_send, y_relay_send, onward_send,
     row_send, row_fwd, row_recv, sib_send, sib_recv, pair_send, pair_recv,
     m_send, m_recv, z_send, z_recv, out_send, out_recv,
 ):
@@ -37,8 +37,12 @@
     chip = col // 2
     z = z_hi * 2 + z_lo
     place = y * 8 + in_plane
-    own_quarter, own_piece = col // 4, lax.rem(col, 4)
-    odd = lax.rem(z_hi, 2)
+    far_y, far_z, next_z, last_z = (
+        lax.rem(y + 2, 4), lax.rem(z_hi + 2, 4), lax.rem(z_hi + 1, 4), lax.rem(z_hi + 3, 4)
+    )
+
+    def opposite(which):
+        return lax.rem(which // 4 + 2, 4) * 4 + lax.rem(which + 2, 4)
 
     def in_plane_id(which):
         return ((which // 8) * 4 + z_hi, z_lo * 8 + lax.rem(which, 8))
@@ -65,10 +69,12 @@
         pl.semaphore_signal(barrier, inc=1, device_id=device_id, device_id_type=MESH)
 
     diagonal = row == col
-    for i in range(2):
-        @pl.when(jnp.logical_not(jnp.logical_and(diagonal, z_hi // 2 == i)))
-        def _(i=i):
-            greet((col, y * 4 + odd + 2 * i))
+
+    @pl.when(jnp.logical_not(diagonal))
+    def _():
+        greet((col, row))
+
+    greet((col, opposite(row)))
 
     @pl.loop(1, 8)
     def _(step):
@@ -105,63 +111,56 @@
 
     pl.semaphore_wait(barrier, 2 + 7 + 3 + 31 - diagonal.astype(jnp.int32))
 
+    def piece(quarter, which):
+        return p_col.at[quarter, pl.ds(pl.multiple_of(64 * which, 64), 64)]
+
+    def arrived(quarter, which):
+        pltpu.make_async_copy(p_own, piece(quarter, which), col_recv.at[quarter, which]).wait()
+
+    own_piece = piece(col // 4, lax.rem(col, 4))
+    own_recv = col_recv.at[col // 4, lax.rem(col, 4)]
+
     def spread(i):
         return pltpu.make_async_remote_copy(
             src_ref=p_own,
-            dst_ref=p_col.at[own_quarter, pl.ds(pl.multiple_of(64 * own_piece, 64), 64)],
+            dst_ref=own_piece,
             send_sem=spread_send.at[i],
-            recv_sem=col_recv.at[own_quarter, own_piece],
-            device_id=(own_quarter * 4 + lax.rem(own_piece, 2) + 2 * i, row),
-            device_id_type=MESH,
-        )
-
-    def spread_self():
-        return pltpu.make_async_copy(
-            p_own,
-            p_col.at[own_quarter, pl.ds(pl.multiple_of(64 * own_piece, 64), 64)],
-            col_recv.at[own_quarter, own_piece],
-        )
-
-    for i in range(2):
-        to_self = jnp.logical_and(diagonal, z_hi // 2 == i)
-
-        @pl.when(to_self)
-        def _():
-            spread_self().start()
-
-        @pl.when(jnp.logical_not(to_self))
-        def _(i=i):
-            spread(i).start()
-
-    pieces = (odd, odd + 2, 1 - odd, 3 - odd)
-
-    def turn(i):
-        which = pieces[i]
-        piece = p_col.at[y, pl.ds(pl.multiple_of(64 * which, 64), 64)]
-        return pltpu.make_async_remote_copy(
-            src_ref=piece,
-            dst_ref=piece,
-            send_sem=turn_send.at[i],
-            recv_sem=col_recv.at[y, which],
-            device_id=(y * 4 + lax.rem(z_hi + 1 + 2 * i, 4), col),
-            device_id_type=MESH,
-        )
-
-    def relay(i, step):
-        which = pieces[i]
-        piece = p_col.at[y, pl.ds(pl.multiple_of(64 * which, 64), 64)]
-        return pltpu.make_async_remote_copy(
-            src_ref=piece,
-            dst_ref=piece,
-            send_sem=relay_send.at[i, step - 1],
-            recv_sem=col_recv.at[y, which],
-            device_id=(lax.rem(y + step, 4) * 4 + z_hi, col),
-            device_id_type=MESH,
-        )
-
-    def arrived(quarter, i):
-        piece = p_col.at[quarter, pl.ds(pl.multiple_of(64 * i, 64), 64)]
-        pltpu.make_async_copy(p_own, piece, col_recv.at[quarter, i]).wait()
+            recv_sem=own_recv,
+            device_id=((col, opposite(col))[i], row),
+            device_id_type=MESH,
+        )
+
+    @pl.when(diagonal)
+    def _():
+        pltpu.make_async_copy(p_own, own_piece, own_recv).start()
+
+    @pl.when(jnp.logical_not(diagonal))
+    def _():
+        spread(0).start()
+
+    spread(1).start()
+
+    held = ((y, z_hi), (far_y, far_z))
+    passed = ((y, last_z), (far_y, next_z))
+
+    def relay(source, send_sem, to_y, to_z):
+        return pltpu.make_async_remote_copy(
+            src_ref=piece(*source),
+            dst_ref=piece(*source),
+            send_sem=send_sem,
+            recv_sem=col_recv.at[source[0], source[1]],
+            device_id=(to_y * 4 + to_z, col),
+            device_id_type=MESH,
+        )
+
+    def along_z(i, step):
+        return relay(held[i], z_relay_send.at[i, step], y, lax.rem(z_hi + step, 4))
+
+    def along_y(i, step):
+        return relay(held[i], y_relay_send.at[i, step], lax.rem(y + step, 4), z_hi)
+
+    def onward(i, step):
+        return relay(passed[i], onward_send.at[i, step], lax.rem(y + step, 4), z_hi)
 
     def to_partner():
         return pltpu.make_async_remote_copy(
@@ -202,19 +201,24 @@
 
     to_partner().start()
     to_sibling(0).start()
-    for i in range(4):
-        arrived(y, pieces[i])
-        if i < 2:
-            turn(i).start()
+    for i in range(2):
+        arrived(*held[i])
+        for step in (1, 3):
+            along_z(i, step).start()
         for step in (2, 1, 3):
-            relay(i, step).start()
-        if i == 1:
-            for step in (2, 1, 3):
-                to_row(0, step).start()
-            row_arrived((1 - z_lo) * 8 + in_plane)
-            for step in (2, 1, 3):
-                to_row(1, step).start()
-            to_sibling(4).start()
+            along_y(i, step).start()
+
+    for step in (2, 1, 3):
+        to_row(0, step).start()
+    row_arrived((1 - z_lo) * 8 + in_plane)
+    for step in (2, 1, 3):
+        to_row(1, step).start()
+    to_sibling(4).start()
+
+    for i in range(2):
+        arrived(*passed[i])
+        for step in (1, 3):
+            onward(i, step).start()
 
     for step in (1, 2, 3, 5, 6, 7):
         row_arrived(lax.rem(chip + step, 8) * 2 + core)
@@ -234,11 +238,10 @@
         pt_t_low[j] = low
 
     total = jnp.zeros((256, 256), F32)
-    for step in (0, 1, 3, 2):
+    for step, rest in ((0, (1, 2)), (2, (0, 3)), (1, (0, 2, 1, 3)), (3, (0, 2, 1, 3))):
         quarter = lax.rem(y + step, 4)
-        if step:
-            for i in range(4):
-                arrived(quarter, i)
+        for i in rest:
+            arrived(quarter, lax.rem(z_hi + i, 4))
         high, low = split(p_col[quarter])
         p_col_high[quarter] = high
         p_col_low[quarter] = low
@@ -361,16 +364,17 @@
     solved_ref[...] = dot3(high, low, d_high[...], d_low[...])
     c_copy.wait()
 
+    @pl.when(jnp.logical_not(diagonal))
+    def _():
+        spread(0).wait_send()
+
+    spread(1).wait_send()
     for i in range(2):
-        @pl.when(jnp.logical_not(jnp.logical_and(diagonal, z_hi // 2 == i)))
-        def _(i=i):
-            spread(i).wait_send()
-
-        turn(i).wait_send()
-
-    for i in range(4):
         for step in (1, 2, 3):
-            relay(i, step).wait_send()
+            along_y(i, step).wait_send()
+        for step in (1, 3):
+            along_z(i, step).wait_send()
+            onward(i, step).wait_send()
     to_sibling(0).wait_send()
     to_partner().wait_send()
     for step in (1, 2, 3):
@@ -438,10 +442,11 @@
             pltpu.VMEM((8, 256), F32),
             pltpu.VMEM((32, 8, 256), F32),
             dma((8,)),
-            dma((4,)),
+            dma((2,)),
             dma((4, 4)),
-            dma((2,)),
-            dma((4, 3)),
+            dma((2, 4)),
+            dma((2, 4)),
+            dma((2, 4)),
             dma((8,)),
             dma((8,)),
             dma((16,)),

time: 57.1 us -> 57.2 us (level)
  no operation moved by 1% of the time
where the time goes in v4:
time: 57.2 us
  Pallas kernels  55.2 us (97%)
  local copies, waits for them, and re-layouts  1.33 us (2%)
  between operations  0.64 us (1%)
    pallas_call x1, Pallas kernels, body(): pl.pallas_call(kernel, out_shape=(jax.ShapeDtypeStruct((64, 256), F32), j...  55.2 us
    unnamed x2, local copies, waits for them, and re-layouts  1.33 us

profile of v4, /device:TPU:1, one launch (start us, length us, event | category | flops | bytes accessed | tf_op | source)
XLA Modules:
  0.0 57.2 jit_solution(9640251346906873795)
XLA Ops:
  0.6 55.2 %adjoint_panel.1 = (f32[64,256]{1,0:T(8,128)S(1)}, f32[256,256]{1,0:T(8,128)S(1)}) custom-call(f32[1024,1024]{1,0:T(8,128)} %t_hbm.1, f32[64,256]{1,0:T(8,128)} %p_hbm.1, f32[64,256]{1,0:T(8,128)} %a_hbm.1, f32[256,256]{1,0:T(8,128)} %d_hbm.1, f32[256,256]{1,0:T(8,128)} %c_hbm.1), custom_call_target="tpu_custom_call" | custom-call | tf_op jit(solution)/shard_map/adjoint_panel/pallas_call | solution.py:408
  55.8 0.6 %copy.9 = f32[64,256]{1,0:T(8,128)} copy(f32[64,256]{1,0:T(8,128)S(1)} %get-tuple-element.4) | data formatting | bytes 131072
  56.5 0.7 %copy.10 = f32[256,256]{1,0:T(8,128)} copy(f32[256,256]{1,0:T(8,128)S(1)} %get-tuple-element.5) | data formatting | bytes 524288

commit v5 on v4

--- a/solution.py
+++ b/solution.py
@@ -26,9 +26,9 @@
     t_hbm, p_hbm, a_hbm, d_hbm, c_hbm, solved_ref, corner_ref,
     t_raw, t_high, t_low, p_own, a_own, d_raw, c_raw, d_high, d_low,
     p_col, p_row, pt_high, pt_low, pt_t_high, pt_t_low, p_col_high, p_col_low, product,
-    sibling, pair_sum, pair_in, m_own, m_in, m_sum, m_plane, md_own, md,
+    sibling, pair_sum, pair_in, x_sum, x_in, m_own, m_in, m_sum, m_plane, md_own, md,
     local_sem, spread_send, col_recv, z_relay_send, y_relay_send, onward_send,
-    row_send, row_fwd, row_recv, sib_send, sib_recv, pair_send, pair_recv,
+    row_send, row_fwd, row_recv, sib_send, sib_recv, pair_send, pair_recv, other_send, other_recv,
     m_send, m_recv, z_send, z_recv, out_send, out_recv,
 ):
     row, col = lax.axis_index("row"), lax.axis_index("col")
@@ -36,7 +36,7 @@
     z_lo, in_plane, core = col // 8, lax.rem(col, 8), lax.rem(col, 2)
     chip = col // 2
     z = z_hi * 2 + z_lo
-    place = y * 8 + in_plane
+    x, place = in_plane // 2, y * 8 + in_plane
     far_y, far_z, next_z, last_z = (
         lax.rem(y + 2, 4), lax.rem(z_hi + 2, 4), lax.rem(z_hi + 1, 4), lax.rem(z_hi + 3, 4)
     )
@@ -80,20 +80,109 @@
     def _(step):
         greet(z_id(lax.rem(z + step, 8)))
 
-    @pl.loop(1, 4)
-    def _(step):
-        greet((row, (1 - z_lo) * 8 + lax.rem(in_plane + 2 * step, 8)))
-
     @pl.loop(1, 32)
     def _(step):
         greet(in_plane_id(lax.rem(place + step, 32)))
 
     p_copy.wait()
+    p_row[col] = p_own[...]
+    pl.semaphore_wait(barrier, 2 + 7 + 31 - diagonal.astype(jnp.int32))
+
+    def piece(quarter, which):
+        return p_col.at[quarter, pl.ds(pl.multiple_of(64 * which, 64), 64)]
+
+    def arrived(quarter, which):
+        pltpu.make_async_copy(p_own, piece(quarter, which), col_recv.at[quarter, which]).wait()
+
+    own_piece = piece(col // 4, lax.rem(col, 4))
+    own_recv = col_recv.at[col // 4, lax.rem(col, 4)]
+
+    def spread(i):
+        return pltpu.make_async_remote_copy(
+            src_ref=p_own,
+            dst_ref=own_piece,
+            send_sem=spread_send.at[i],
+            recv_sem=own_recv,
+            device_id=((col, opposite(col))[i], row),
+            device_id_type=MESH,
+        )
+
+    @pl.when(diagonal)
+    def _():
+        pltpu.make_async_copy(p_own, own_piece, own_recv).start()
+
+    @pl.when(jnp.logical_not(diagonal))
+    def _():
+        spread(0).start()
+
+    spread(1).start()
+
+    held = ((y, z_hi), (far_y, far_z))
+    passed = ((y, last_z), (far_y, next_z))
+
+    def relay(source, send_sem, to_y, to_z):
+        return pltpu.make_async_remote_copy(
+            src_ref=piece(*source),
+            dst_ref=piece(*source),
+            send_sem=send_sem,
+            recv_sem=col_recv.at[source[0], source[1]],
+            device_id=(to_y * 4 + to_z, col),
+            device_id_type=MESH,
+        )
+
+    def along_z(i, step):
+        return relay(held[i], z_relay_send.at[i, step], y, lax.rem(z_hi + step, 4))
+
+    def along_y(i, step):
+        return relay(held[i], y_relay_send.at[i, step], lax.rem(y + step, 4), z_hi)
+
+    def onward(i, step):
+        return relay(passed[i], onward_send.at[i, step], lax.rem(y + step, 4), z_hi)
+
+    def to_partner():
+        return pltpu.make_async_remote_copy(
+            src_ref=p_own,
+            dst_ref=p_row.at[col],
+            send_sem=row_send.at[0],
+            recv_sem=row_recv.at[col],
+            device_id=(row, (1 - z_lo) * 8 + in_plane),
+            device_id_type=MESH,
+        )
+
+    def to_row(half, step):
+        which = lax.rem(z_lo + half, 2) * 8 + in_plane
+        block = p_row.at[which]
+        return pltpu.make_async_remote_copy(
+            src_ref=block,
+            dst_ref=block,
+            send_sem=row_send.at[half * 4 + step],
+            recv_sem=row_recv.at[which],
+            device_id=(row, z_lo * 8 + lax.rem(in_plane + 2 * step, 8)),
+            device_id_type=MESH,
+        )
+
+    def to_sibling(step):
+        which = lax.rem(chip + step, 8) * 2 + core
+        block = p_row.at[which]
+        return pltpu.make_async_remote_copy(
+            src_ref=block,
+            dst_ref=block,
+            send_sem=row_fwd.at[step],
+            recv_sem=row_recv.at[which],
+            device_id=(row, chip * 2 + 1 - core),
+            device_id_type=MESH,
+        )
+
+    def row_arrived(which):
+        pltpu.make_async_copy(p_own, p_row.at[which], row_recv.at[which]).wait()
+
+    to_partner().start()
+    to_sibling(0).start()
+
     a_copy.wait()
     p_high, p_low = split(p_own[...])
     a_high, a_low = split(a_own[...])
     m_own[...] = dot3(p_high.T, p_low.T, a_high, a_low).reshape(32, 8, 256)
-    p_row[col] = p_own[...]
     for i in range(4):
         slabs[i].wait()
 
@@ -109,111 +198,19 @@
     d_high[...] = high
     d_low[...] = low
 
-    pl.semaphore_wait(barrier, 2 + 7 + 3 + 31 - diagonal.astype(jnp.int32))
-
-    def piece(quarter, which):
-        return p_col.at[quarter, pl.ds(pl.multiple_of(64 * which, 64), 64)]
-
-    def arrived(quarter, which):
-        pltpu.make_async_copy(p_own, piece(quarter, which), col_recv.at[quarter, which]).wait()
-
-    own_piece = piece(col // 4, lax.rem(col, 4))
-    own_recv = col_recv.at[col // 4, lax.rem(col, 4)]
-
-    def spread(i):
-        return pltpu.make_async_remote_copy(
-            src_ref=p_own,
-            dst_ref=own_piece,
-            send_sem=spread_send.at[i],
-            recv_sem=own_recv,
-            device_id=((col, opposite(col))[i], row),
-            device_id_type=MESH,
-        )
-
-    @pl.when(diagonal)
-    def _():
-        pltpu.make_async_copy(p_own, own_piece, own_recv).start()
-
-    @pl.when(jnp.logical_not(diagonal))
-    def _():
-        spread(0).start()
-
-    spread(1).start()
-
-    held = ((y, z_hi), (far_y, far_z))
-    passed = ((y, last_z), (far_y, next_z))
-
-    def relay(source, send_sem, to_y, to_z):
-        return pltpu.make_async_remote_copy(
-            src_ref=piece(*source),
-            dst_ref=piece(*source),
-            send_sem=send_sem,
-            recv_sem=col_recv.at[source[0], source[1]],
-            device_id=(to_y * 4 + to_z, col),
-            device_id_type=MESH,
-        )
-
-    def along_z(i, step):
-        return relay(held[i], z_relay_send.at[i, step], y, lax.rem(z_hi + step, 4))
-
-    def along_y(i, step):
-        return relay(held[i], y_relay_send.at[i, step], lax.rem(y + step, 4), z_hi)
-
-    def onward(i, step):
-        return relay(passed[i], onward_send.at[i, step], lax.rem(y + step, 4), z_hi)
-
-    def to_partner():
-        return pltpu.make_async_remote_copy(
-            src_ref=p_own,
-            dst_ref=p_row.at[col],
-            send_sem=row_send.at[0],
-            recv_sem=row_recv.at[col],
-            device_id=(row, (1 - z_lo) * 8 + in_plane),
-            device_id_type=MESH,
-        )
-
-    def to_row(half, step):
-        which = lax.rem(z_lo + half, 2) * 8 + in_plane
-        block = p_row.at[which]
-        return pltpu.make_async_remote_copy(
-            src_ref=block,
-            dst_ref=block,
-            send_sem=row_send.at[half * 4 + step],
-            recv_sem=row_recv.at[which],
-            device_id=(row, z_lo * 8 + lax.rem(in_plane + 2 * step, 8)),
-            device_id_type=MESH,
-        )
-
-    def to_sibling(step):
-        which = lax.rem(chip + step, 8) * 2 + core
-        block = p_row.at[which]
-        return pltpu.make_async_remote_copy(
-            src_ref=block,
-            dst_ref=block,
-            send_sem=row_fwd.at[step],
-            recv_sem=row_recv.at[which],
-            device_id=(row, chip * 2 + 1 - core),
-            device_id_type=MESH,
-        )
-
-    def row_arrived(which):
-        pltpu.make_async_copy(p_own, p_row.at[which], row_recv.at[which]).wait()
-
-    to_partner().start()
-    to_sibling(0).start()
+    for step in (2, 1, 3):
+        to_row(0, step).start()
+    row_arrived((1 - z_lo) * 8 + in_plane)
+    for step in (2, 1, 3):
+        to_row(1, step).start()
+    to_sibling(4).start()
+
     for i in range(2):
         arrived(*held[i])
         for step in (1, 3):
             along_z(i, step).start()
         for step in (2, 1, 3):
             along_y(i, step).start()
-
-    for step in (2, 1, 3):
-        to_row(0, step).start()
-    row_arrived((1 - z_lo) * 8 + in_plane)
-    for step in (2, 1, 3):
-        to_row(1, step).start()
-    to_sibling(4).start()
 
     for i in range(2):
         arrived(*passed[i])
@@ -285,16 +282,19 @@
     for i in range(8):
         pair_sum[i] = product[i, core] + sibling[i]
 
-    def to_chip(step):
-        which = lax.rem(chip + step, 8)
-        return pltpu.make_async_remote_copy(
-            src_ref=pair_sum.at[which],
-            dst_ref=pair_in.at[chip],
-            send_sem=pair_send.at[step],
-            recv_sem=pair_recv.at[chip],
-            device_id=(row, which * 2 + core),
-            device_id_type=MESH,
-        )
+    def to_chip(step, half):
+        return pltpu.make_async_remote_copy(
+            src_ref=pair_sum.at[half * 4 + lax.rem(x + step, 4)],
+            dst_ref=pair_in.at[half * 4 + x],
+            send_sem=pair_send.at[half * 4 + step],
+            recv_sem=pair_recv.at[half * 4 + x],
+            device_id=(row, z_lo * 8 + lax.rem(in_plane + 2 * step, 8)),
+            device_id_type=MESH,
+        )
+
+    for half in range(2):
+        for step in (2, 1, 3):
+            to_chip(step, half).start()
 
     @pl.loop(1, 32)
     def _(step):
@@ -320,10 +320,6 @@
     @pl.loop(1, 8)
     def _(step):
         to_z(step).start()
-
-    @pl.loop(1, 8)
-    def _(step):
-        to_chip(step).start()
 
     @pl.loop(1, 8)
     def _(step):
@@ -352,14 +348,26 @@
     def _(step):
         to_all(step).start()
 
-    @pl.loop(1, 8)
-    def _(step):
-        which = lax.rem(chip + step, 8)
-        pltpu.make_async_copy(p_own, pair_in.at[which], pair_recv.at[which]).wait()
-
-    reduced = pair_sum[chip]
-    for step in range(1, 8):
-        reduced += pair_in[lax.rem(chip + step, 8)]
+    for half in range(2):
+        for step in (1, 2, 3):
+            which = half * 4 + lax.rem(x + step, 4)
+            pltpu.make_async_copy(p_own, pair_in.at[which], pair_recv.at[which]).wait()
+        reduced = pair_sum[half * 4 + x]
+        for step in (1, 2, 3):
+            reduced += pair_in[half * 4 + lax.rem(x + step, 4)]
+        x_sum[half] = reduced
+
+    to_other = pltpu.make_async_remote_copy(
+        src_ref=x_sum.at[1 - z_lo],
+        dst_ref=x_in,
+        send_sem=other_send,
+        recv_sem=other_recv,
+        device_id=(row, (1 - z_lo) * 8 + in_plane),
+        device_id_type=MESH,
+    )
+    to_other.start()
+    to_other.wait_recv()
+    reduced = x_sum[z_lo] + x_in[...]
     high, low = split(a_own[...] - 2.0 * reduced)
     solved_ref[...] = dot3(high, low, d_high[...], d_low[...])
     c_copy.wait()
@@ -381,11 +389,14 @@
         to_row(0, step).wait_send()
         to_row(1, step).wait_send()
     to_pair.wait_send()
+    to_other.wait_send()
+    for step in (1, 2, 3):
+        to_chip(step, 0).wait_send()
+        to_chip(step, 1).wait_send()
 
     @pl.loop(1, 8)
     def _(step):
         to_sibling(step).wait_send()
-        to_chip(step).wait_send()
         to_z(step).wait_send()
 
     @pl.loop(1, 32)
@@ -435,6 +446,8 @@
             pltpu.VMEM((8, 64, 256), F32),
             pltpu.VMEM((8, 64, 256), F32),
             pltpu.VMEM((8, 64, 256), F32),
+            pltpu.VMEM((2, 64, 256), F32),
+            pltpu.VMEM((64, 256), F32),
             pltpu.VMEM((32, 8, 256), F32),
             pltpu.VMEM((32, 8, 256), F32),
             pltpu.VMEM((8, 256), F32),
@@ -454,6 +467,8 @@
             dma(()),
             dma((8,)),
             dma((8,)),
+            dma(()),
+            dma(()),
             dma((32,)),
             dma((32,)),
             dma((8,)),

time: 57.2 us -> 54.6 us (0.955)
  Pallas kernels: 55.2 us -> 52.5 us
    pallas_call x1, Pallas kernels: 55.2 us -> 52.5 us  [body(): pl.pallas_call(kernel, out_shape=(jax.ShapeDtypeStruct((64, 256), F32), j...]
where the time goes in v5:
time: 54.6 us; the launch traced here: 54.5 us
  Pallas kernels  52.5 us (96%)
  local copies, waits for them, and re-layouts  1.33 us (2%)
  between operations  0.64 us (1%)
    pallas_call x1, Pallas kernels, body(): pl.pallas_call(kernel, out_shape=(jax.ShapeDtypeStruct((64, 256), F32), j...  52.5 us
    unnamed x2, local copies, waits for them, and re-layouts  1.33 us

profile of v5, /device:TPU:1, one launch (start us, length us, event | category | flops | bytes accessed | tf_op | source)
XLA Modules:
  0.0 54.5 jit_solution(9624371804365805045)
XLA Ops:
  0.6 52.5 %adjoint_panel.1 = (f32[64,256]{1,0:T(8,128)S(1)}, f32[256,256]{1,0:T(8,128)S(1)}) custom-call(f32[1024,1024]{1,0:T(8,128)} %t_hbm.1, f32[64,256]{1,0:T(8,128)} %p_hbm.1, f32[64,256]{1,0:T(8,128)} %a_hbm.1, f32[256,256]{1,0:T(8,128)} %d_hbm.1, f32[256,256]{1,0:T(8,128)} %c_hbm.1), custom_call_target="tpu_custom_call" | custom-call | tf_op jit(solution)/shard_map/adjoint_panel/pallas_call | solution.py:419
  53.2 0.6 %copy.9 = f32[64,256]{1,0:T(8,128)} copy(f32[64,256]{1,0:T(8,128)S(1)} %get-tuple-element.4) | data formatting | bytes 131072
  53.8 0.7 %copy.10 = f32[256,256]{1,0:T(8,128)} copy(f32[256,256]{1,0:T(8,128)S(1)} %get-tuple-element.5) | data formatting | bytes 524288

commit v6 on v5

--- a/solution.py
+++ b/solution.py
@@ -32,23 +32,35 @@
     m_send, m_recv, z_send, z_recv, out_send, out_recv,
 ):
     row, col = lax.axis_index("row"), lax.axis_index("col")
-    y, z_hi = row // 4, lax.rem(row, 4)
-    z_lo, in_plane, core = col // 8, lax.rem(col, 8), lax.rem(col, 2)
-    chip = col // 2
+    y, z_hi = lax.div(row, 4), lax.rem(row, 4)
+    z_lo, in_plane, core = lax.div(col, 8), lax.rem(col, 8), lax.rem(col, 2)
+    chip = lax.div(col, 2)
     z = z_hi * 2 + z_lo
-    x, place = in_plane // 2, y * 8 + in_plane
+    x, place = lax.div(in_plane, 2), y * 8 + in_plane
     far_y, far_z, next_z, last_z = (
         lax.rem(y + 2, 4), lax.rem(z_hi + 2, 4), lax.rem(z_hi + 1, 4), lax.rem(z_hi + 3, 4)
     )
 
     def opposite(which):
-        return lax.rem(which // 4 + 2, 4) * 4 + lax.rem(which + 2, 4)
-
-    def in_plane_id(which):
-        return ((which // 8) * 4 + z_hi, z_lo * 8 + lax.rem(which, 8))
-
-    def z_id(which):
-        return (y * 4 + which // 2, lax.rem(which, 2) * 8 + in_plane)
+        return lax.rem(lax.div(which, 4) + 2, 4) * 4 + lax.rem(which + 2, 4)
+
+    rows = [lax.rem(y + step, 4) for step in range(4)]
+    places = [lax.rem(in_plane + step, 8) for step in range(8)]
+    plane = [
+        (rows[i] * 8 + places[j], (rows[i] * 4 + z_hi, z_lo * 8 + places[j]))
+        for i in (2, 1, 3, 0)
+        for j in (4, 5, 3, 2, 6, 1, 7, 0)
+        if i or j
+    ]
+    along_z_ids = []
+    for step in (4, 3, 5, 2, 6, 1, 7):
+        to_z = lax.rem(z + step, 8)
+        along_z_ids.append((y * 4 + lax.div(to_z, 2), lax.rem(to_z, 2) * 8 + in_plane))
+
+    def whole(pieces, count, sem):
+        pltpu.make_async_copy(
+            pieces.at[pl.ds(0, count)], pieces.at[pl.ds(0, count)], sem
+        ).wait()
 
     slabs = [
         pltpu.make_async_copy(
@@ -76,13 +88,11 @@
 
     greet((col, opposite(row)))
 
-    @pl.loop(1, 8)
-    def _(step):
-        greet(z_id(lax.rem(z + step, 8)))
-
-    @pl.loop(1, 32)
-    def _(step):
-        greet(in_plane_id(lax.rem(place + step, 32)))
+    for device_id in along_z_ids:
+        greet(device_id)
+
+    for _, device_id in plane:
+        greet(device_id)
 
     p_copy.wait()
     p_row[col] = p_own[...]
@@ -94,8 +104,8 @@
     def arrived(quarter, which):
         pltpu.make_async_copy(p_own, piece(quarter, which), col_recv.at[quarter, which]).wait()
 
-    own_piece = piece(col // 4, lax.rem(col, 4))
-    own_recv = col_recv.at[col // 4, lax.rem(col, 4)]
+    own_piece = piece(lax.div(col, 4), lax.rem(col, 4))
+    own_recv = col_recv.at[lax.div(col, 4), lax.rem(col, 4)]
 
     def spread(i):
         return pltpu.make_async_remote_copy(
@@ -246,20 +256,15 @@
     m_own[...] = m_own[...] - 2.0 * total.reshape(32, 8, 256)
     m_in[place] = m_own[place]
 
-    def to_plane(step):
-        which = lax.rem(place + step, 32)
-        return pltpu.make_async_remote_copy(
+    for which, device_id in plane:
+        pltpu.make_async_remote_copy(
             src_ref=m_own.at[which],
             dst_ref=m_in.at[place],
-            send_sem=m_send.at[step],
-            recv_sem=m_recv.at[place],
-            device_id=in_plane_id(which),
-            device_id_type=MESH,
-        )
-
-    @pl.loop(1, 32)
-    def _(step):
-        to_plane(step).start()
+            send_sem=m_send,
+            recv_sem=m_recv,
+            device_id=device_id,
+            device_id_type=MESH,
+        ).start()
 
     @pl.loop(0, 4)
     def _(i):
@@ -296,10 +301,7 @@
         for step in (2, 1, 3):
             to_chip(step, half).start()
 
-    @pl.loop(1, 32)
-    def _(step):
-        which = lax.rem(place + step, 32)
-        pltpu.make_async_copy(md_own, m_in.at[which], m_recv.at[which]).wait()
+    whole(m_in, 31, m_recv)
 
     total = m_in[0]
     for i in range(1, 32):
@@ -307,24 +309,17 @@
     m_sum[...] = total
     m_plane[z] = total
 
-    def to_z(step):
-        return pltpu.make_async_remote_copy(
+    for device_id in along_z_ids:
+        pltpu.make_async_remote_copy(
             src_ref=m_sum,
             dst_ref=m_plane.at[z],
-            send_sem=z_send.at[step],
-            recv_sem=z_recv.at[z],
-            device_id=z_id(lax.rem(z + step, 8)),
-            device_id_type=MESH,
-        )
-
-    @pl.loop(1, 8)
-    def _(step):
-        to_z(step).start()
-
-    @pl.loop(1, 8)
-    def _(step):
-        which = lax.rem(z + step, 8)
-        pltpu.make_async_copy(md_own, m_plane.at[which], z_recv.at[which]).wait()
+            send_sem=z_send,
+            recv_sem=z_recv,
+            device_id=device_id,
+            device_id_type=MESH,
+        ).start()
+
+    whole(m_plane, 7, z_recv)
 
     total = m_plane[0]
     for i in range(1, 8):
@@ -334,19 +329,15 @@
     md_own[...] = total
     md[place] = total
 
-    def to_all(step):
-        return pltpu.make_async_remote_copy(
+    for _, device_id in plane:
+        pltpu.make_async_remote_copy(
             src_ref=md_own,
             dst_ref=md.at[place],
-            send_sem=out_send.at[step],
-            recv_sem=out_recv.at[place],
-            device_id=in_plane_id(lax.rem(place + step, 32)),
-            device_id_type=MESH,
-        )
-
-    @pl.loop(1, 32)
-    def _(step):
-        to_all(step).start()
+            send_sem=out_send,
+            recv_sem=out_recv,
+            device_id=device_id,
+            device_id_type=MESH,
+        ).start()
 
     for half in range(2):
         for step in (1, 2, 3):
@@ -397,17 +388,12 @@
     @pl.loop(1, 8)
     def _(step):
         to_sibling(step).wait_send()
-        to_z(step).wait_send()
-
-    @pl.loop(1, 32)
-    def _(step):
-        to_plane(step).wait_send()
-        to_all(step).wait_send()
-
-    @pl.loop(1, 32)
-    def _(step):
-        which = lax.rem(place + step, 32)
-        pltpu.make_async_copy(md_own, md.at[which], out_recv.at[which]).wait()
+
+    whole(m_in, 31, m_send)
+    whole(m_plane, 7, z_send)
+    whole(md, 31, out_send)
+
+    whole(md, 31, out_recv)
 
     corner_ref[...] = c_raw[...] - md[...].reshape(256, 256).T
 
@@ -469,12 +455,12 @@
             dma((8,)),
             dma(()),
             dma(()),
-            dma((32,)),
-            dma((32,)),
-            dma((8,)),
-            dma((8,)),
-            dma((32,)),
-            dma((32,)),
+            dma(()),
+            dma(()),
+            dma(()),
+            dma(()),
+            dma(()),
+            dma(()),
         ],
         compiler_params=pltpu.CompilerParams(
             collective_id=0, has_side_effects=True, vmem_limit_bytes=32 * 1024 * 1024

time: 54.6 us -> 51.5 us (0.943)
  Pallas kernels: 52.5 us -> 49.4 us
    pallas_call x1, Pallas kernels: 52.5 us -> 49.4 us  [body(): pl.pallas_call(kernel, out_shape=(jax.ShapeDtypeStruct((64, 256), F32), j...]
where the time goes in v6:
time: 51.5 us; the launch traced here: 51.4 us
  Pallas kernels  49.4 us (96%)
  local copies, waits for them, and re-layouts  1.33 us (3%)
  between operations  0.64 us (1%)
    pallas_call x1, Pallas kernels, body(): pl.pallas_call(kernel, out_shape=(jax.ShapeDtypeStruct((64, 256), F32), j...  49.4 us
    unnamed x2, local copies, waits for them, and re-layouts  1.33 us

profile of v6, /device:TPU:1, one launch (start us, length us, event | category | flops | bytes accessed | tf_op | source)
XLA Modules:
  0.0 51.4 jit_solution(17857159154859746585)
XLA Ops:
  0.6 49.4 %adjoint_panel.1 = (f32[64,256]{1,0:T(8,128)S(1)}, f32[256,256]{1,0:T(8,128)S(1)}) custom-call(f32[1024,1024]{1,0:T(8,128)} %t_hbm.1, f32[64,256]{1,0:T(8,128)} %p_hbm.1, f32[64,256]{1,0:T(8,128)} %a_hbm.1, f32[256,256]{1,0:T(8,128)} %d_hbm.1, f32[256,256]{1,0:T(8,128)} %c_hbm.1), custom_call_target="tpu_custom_call" | custom-call | tf_op jit(solution)/shard_map/adjoint_panel/pallas_call | solution.py:405
  50.1 0.6 %copy.9 = f32[64,256]{1,0:T(8,128)} copy(f32[64,256]{1,0:T(8,128)S(1)} %get-tuple-element.4) | data formatting | bytes 131072
  50.7 0.7 %copy.10 = f32[256,256]{1,0:T(8,128)} copy(f32[256,256]{1,0:T(8,128)S(1)} %get-tuple-element.5) | data formatting | bytes 524288

commit v7 on v6

--- a/solution.py
+++ b/solution.py
@@ -27,7 +27,7 @@
     t_raw, t_high, t_low, p_own, a_own, d_raw, c_raw, d_high, d_low,
     p_col, p_row, pt_high, pt_low, pt_t_high, pt_t_low, p_col_high, p_col_low, product,
     sibling, pair_sum, pair_in, x_sum, x_in, m_own, m_in, m_sum, m_plane, md_own, md,
-    local_sem, spread_send, col_recv, z_relay_send, y_relay_send, onward_send,
+    local_sem, spread_send, col_recv, z_relay_send, y_relay_send, onward_send, across_send,
     row_send, row_fwd, row_recv, sib_send, sib_recv, pair_send, pair_recv, other_send, other_recv,
     m_send, m_recv, z_send, z_recv, out_send, out_recv,
 ):
@@ -96,6 +96,19 @@
 
     p_copy.wait()
     p_row[col] = p_own[...]
+    def split_slab(i):
+        slabs[i].wait()
+
+        @pl.loop(0, 4)
+        def _(j):
+            rows = pl.ds(256 * i, 256)
+            high, low = split(t_raw[rows, pl.ds(pl.multiple_of(256 * j, 256), 256)])
+            t_high[j, rows] = high
+            t_low[j, rows] = low
+
+    split_slab(0)
+    split_slab(1)
+
     pl.semaphore_wait(barrier, 2 + 7 + 31 - diagonal.astype(jnp.int32))
 
     def piece(quarter, which):
@@ -129,6 +142,7 @@
 
     held = ((y, z_hi), (far_y, far_z))
     passed = ((y, last_z), (far_y, next_z))
+    beside = ((rows[3], z_hi), (rows[3], far_z))
 
     def relay(source, send_sem, to_y, to_z):
         return pltpu.make_async_remote_copy(
@@ -145,6 +159,9 @@
 
     def along_y(i, step):
         return relay(held[i], y_relay_send.at[i, step], lax.rem(y + step, 4), z_hi)
+
+    def across(i):
+        return relay(beside[i], across_send.at[i], lax.rem(y + 1 + 2 * i, 4), z_hi)
 
     def onward(i, step):
         return relay(passed[i], onward_send.at[i, step], lax.rem(y + step, 4), z_hi)
@@ -189,24 +206,8 @@
     to_partner().start()
     to_sibling(0).start()
 
-    a_copy.wait()
-    p_high, p_low = split(p_own[...])
-    a_high, a_low = split(a_own[...])
-    m_own[...] = dot3(p_high.T, p_low.T, a_high, a_low).reshape(32, 8, 256)
-    for i in range(4):
-        slabs[i].wait()
-
-        @pl.loop(0, 4)
-        def _(j, i=i):
-            rows = pl.ds(256 * i, 256)
-            high, low = split(t_raw[rows, pl.ds(pl.multiple_of(256 * j, 256), 256)])
-            t_high[j, rows] = high
-            t_low[j, rows] = low
-
-    d_copy.wait()
-    high, low = split(d_raw[...])
-    d_high[...] = high
-    d_low[...] = low
+    split_slab(2)
+    split_slab(3)
 
     for step in (2, 1, 3):
         to_row(0, step).start()
@@ -219,13 +220,22 @@
         arrived(*held[i])
         for step in (1, 3):
             along_z(i, step).start()
-        for step in (2, 1, 3):
+        for step in (1, 3):
             along_y(i, step).start()
+
+    for i in range(2):
+        arrived(*beside[i])
+        across(i).start()
 
     for i in range(2):
         arrived(*passed[i])
         for step in (1, 3):
             onward(i, step).start()
+
+    a_copy.wait()
+    p_high, p_low = split(p_own[...])
+    a_high, a_low = split(a_own[...])
+    m_own[...] = dot3(p_high.T, p_low.T, a_high, a_low).reshape(32, 8, 256)
 
     for step in (1, 2, 3, 5, 6, 7):
         row_arrived(lax.rem(chip + step, 8) * 2 + core)
@@ -245,7 +255,7 @@
         pt_t_low[j] = low
 
     total = jnp.zeros((256, 256), F32)
-    for step, rest in ((0, (1, 2)), (2, (0, 3)), (1, (0, 2, 1, 3)), (3, (0, 2, 1, 3))):
+    for step, rest in ((0, (1, 2)), (2, (0, 3)), (1, (0, 2, 1, 3)), (3, (1, 3))):
         quarter = lax.rem(y + step, 4)
         for i in rest:
             arrived(quarter, lax.rem(z_hi + i, 4))
@@ -273,6 +283,11 @@
         for j in range(4):
             total += dot3(t_high[j, rows], t_low[j, rows], p_col_high[j], p_col_low[j])
         product[pl.ds(2 * i, 2)] = total.reshape(2, 2, 64, 256)
+
+    d_copy.wait()
+    high, low = split(d_raw[...])
+    d_high[...] = high
+    d_low[...] = low
 
     to_pair = pltpu.make_async_remote_copy(
         src_ref=product.at[:, 1 - core],
@@ -369,9 +384,9 @@
 
     spread(1).wait_send()
     for i in range(2):
-        for step in (1, 2, 3):
+        across(i).wait_send()
+        for step in (1, 3):
             along_y(i, step).wait_send()
-        for step in (1, 3):
             along_z(i, step).wait_send()
             onward(i, step).wait_send()
     to_sibling(0).wait_send()
@@ -398,11 +413,20 @@
     corner_ref[...] = c_raw[...] - md[...].reshape(256, 256).T
 
 
+def store(solved_ref, corner_ref, solved_out, corner_out, solved_sem, corner_sem):
+    corner = pltpu.make_async_copy(corner_ref, corner_out, corner_sem)
+    solved = pltpu.make_async_copy(solved_ref, solved_out, solved_sem)
+    corner.start()
+    solved.start()
+    corner.wait()
+    solved.wait()
+
+
 def body(*arrays):
     hbm = pl.BlockSpec(memory_space=pltpu.HBM)
     vmem = pl.BlockSpec(memory_space=pltpu.VMEM)
     dma = pltpu.SemaphoreType.DMA
-    return pl.pallas_call(
+    results = pl.pallas_call(
         kernel,
         out_shape=(
             jax.ShapeDtypeStruct((64, 256), F32),
@@ -446,6 +470,7 @@
             dma((2, 4)),
             dma((2, 4)),
             dma((2, 4)),
+            dma((2,)),
             dma((8,)),
             dma((8,)),
             dma((16,)),
@@ -467,6 +492,17 @@
         ),
         name="adjoint_panel",
     )(*(pltpu.with_memory_space_constraint(x, pltpu.HBM) for x in arrays))
+    return pl.pallas_call(
+        store,
+        out_shape=(
+            jax.ShapeDtypeStruct((64, 256), F32),
+            jax.ShapeDtypeStruct((256, 256), F32),
+        ),
+        in_specs=[pl.BlockSpec(memory_space=pl.ANY)] * 2,
+        out_specs=(hbm, hbm),
+        scratch_shapes=[dma(()), dma(())],
+        name="store_results",
+    )(*results)
 
 
 def solution(mesh):

time: 51.5 us -> 62.8 us (1.22)
  Pallas kernels: 49.4 us -> 60.8 us
    pallas_call x0 -> x1, Pallas kernels: none -> 11 us  [body(): pl.pallas_call(store, out_shape=(jax.ShapeDtypeStruct((64, 256), F32), ja...]
    unnamed x2 -> x4, local copies, waits for them, and re-layouts: 1.33 us -> 1.31 us
where the time goes in v7:
time: 62.8 us
  Pallas kernels  60.8 us (97%)
  local copies, waits for them, and re-layouts  1.31 us (2%)
  between operations  0.65 us (1%)
    pallas_call x1, Pallas kernels, body(): pl.pallas_call(kernel, out_shape=(jax.ShapeDtypeStruct((64, 256), F32), j...  49.8 us
    pallas_call x1, Pallas kernels, body(): pl.pallas_call(store, out_shape=(jax.ShapeDtypeStruct((64, 256), F32), ja...  11 us
    unnamed x4, local copies, waits for them, and re-layouts  1.31 us

profile of v7, /device:TPU:1, one launch (start us, length us, event | category | flops | bytes accessed | tf_op | source)
XLA Modules:
  0.0 62.8 jit_solution(9496596358842942401)
XLA Ops:
  0.6 49.8 %adjoint_panel.1 = (f32[64,256]{1,0:T(8,128)S(1)}, f32[256,256]{1,0:T(8,128)S(1)}) custom-call(f32[1024,1024]{1,0:T(8,128)} %t_hbm.1, f32[64,256]{1,0:T(8,128)} %p_hbm.1, f32[64,256]{1,0:T(8,128)} %a_hbm.1, f32[256,256]{1,0:T(8,128)} %d_hbm.1, f32[256,256]{1,0:T(8,128)} %c_hbm.1), custom_call_target="tpu_custom_call" | custom-call | tf_op jit(solution)/shard_map/adjoint_panel/pallas_call | solution.py:429
  50.4 0.0 copy-start
  50.4 0.7 %copy-done = f32[256,256]{1,0:T(8,128)} copy-done((f32[256,256]{1,0:T(8,128)}, f32[256,256]{1,0:T(8,128)S(1)}, u32[]{:S(2)}) %copy-start) | copy-done | bytes 262168
  51.1 0.0 copy-start.1
  51.1 0.6 %copy-done.1 = f32[64,256]{1,0:T(8,128)} copy-done((f32[64,256]{1,0:T(8,128)}, f32[64,256]{1,0:T(8,128)S(1)}, u32[]{:S(2)}) %copy-start.1) | copy-done | bytes 65560
  51.7 11.0 %store_results.1 = (f32[64,256]{1,0:T(8,128)}, f32[256,256]{1,0:T(8,128)}) custom-call(f32[64,256]{1,0:T(8,128)} %copy-done.1, f32[256,256]{1,0:T(8,128)} %copy-done), custom_call_target="tpu_custom_call" | custom-call | tf_op jit(solution)/shard_map/store_results/pallas_call | solution.py:495
Async XLA Ops:
  50.4 0.7 %copy-start = (f32[256,256]{1,0:T(8,128)}, f32[256,256]{1,0:T(8,128)S(1)}, u32[]{:S(2)}) copy-start(f32[256,256]{1,0:T(8,128)S(1)} %get-tuple-element.5.corner_ref) | copy-start | bytes 786436
  51.1 0.6 %copy-start.1 = (f32[64,256]{1,0:T(8,128)}, f32[64,256]{1,0:T(8,128)S(1)}, u32[]{:S(2)}) copy-start(f32[64,256]{1,0:T(8,128)S(1)} %get-tuple-element.4.solved_ref) | copy-start | bytes 196612

commit v8 on v6

--- a/solution.py
+++ b/solution.py
@@ -266,6 +266,16 @@
             device_id_type=MESH,
         ).start()
 
+    def to_pair(i):
+        return pltpu.make_async_remote_copy(
+            src_ref=product.at[pl.ds(2 * i, 2), 1 - core],
+            dst_ref=sibling.at[pl.ds(2 * i, 2)],
+            send_sem=sib_send.at[i],
+            recv_sem=sib_recv.at[i],
+            device_id=(row, chip * 2 + 1 - core),
+            device_id_type=MESH,
+        )
+
     @pl.loop(0, 4)
     def _(i):
         rows = pl.ds(pl.multiple_of(256 * i, 256), 256)
@@ -273,19 +283,12 @@
         for j in range(4):
             total += dot3(t_high[j, rows], t_low[j, rows], p_col_high[j], p_col_low[j])
         product[pl.ds(2 * i, 2)] = total.reshape(2, 2, 64, 256)
-
-    to_pair = pltpu.make_async_remote_copy(
-        src_ref=product.at[:, 1 - core],
-        dst_ref=sibling,
-        send_sem=sib_send,
-        recv_sem=sib_recv,
-        device_id=(row, chip * 2 + 1 - core),
-        device_id_type=MESH,
-    )
-    to_pair.start()
-    to_pair.wait_recv()
-    for i in range(8):
-        pair_sum[i] = product[i, core] + sibling[i]
+        to_pair(i).start()
+
+    for i in range(4):
+        to_pair(i).wait_recv()
+        for j in (2 * i, 2 * i + 1):
+            pair_sum[j] = product[j, core] + sibling[j]
 
     def to_chip(step, half):
         return pltpu.make_async_remote_copy(
@@ -379,7 +382,8 @@
     for step in (1, 2, 3):
         to_row(0, step).wait_send()
         to_row(1, step).wait_send()
-    to_pair.wait_send()
+    for i in range(4):
+        to_pair(i).wait_send()
     to_other.wait_send()
     for step in (1, 2, 3):
         to_chip(step, 0).wait_send()
@@ -449,8 +453,8 @@
             dma((8,)),
             dma((8,)),
             dma((16,)),
-            dma(()),
-            dma(()),
+            dma((4,)),
+            dma((4,)),
             dma((8,)),
             dma((8,)),
             dma(()),

time: 51.5 us -> 51.5 us (level)
  no operation moved by 1% of the time
where the time goes in v8:
time: 51.5 us
  Pallas kernels  49.5 us (96%)
  local copies, waits for them, and re-layouts  1.33 us (3%)
  between operations  0.64 us (1%)
    pallas_call x1, Pallas kernels, body(): pl.pallas_call(kernel, out_shape=(jax.ShapeDtypeStruct((64, 256), F32), j...  49.5 us
    unnamed x2, local copies, waits for them, and re-layouts  1.33 us

profile of v8, /device:TPU:1, one launch (start us, length us, event | category | flops | bytes accessed | tf_op | source)
XLA Modules:
  0.0 51.5 jit_solution(4383769328337182003)
XLA Ops:
  0.6 49.5 %adjoint_panel.1 = (f32[64,256]{1,0:T(8,128)S(1)}, f32[256,256]{1,0:T(8,128)S(1)}) custom-call(f32[1024,1024]{1,0:T(8,128)} %t_hbm.1, f32[64,256]{1,0:T(8,128)} %p_hbm.1, f32[64,256]{1,0:T(8,128)} %a_hbm.1, f32[256,256]{1,0:T(8,128)} %d_hbm.1, f32[256,256]{1,0:T(8,128)} %c_hbm.1), custom_call_target="tpu_custom_call" | custom-call | tf_op jit(solution)/shard_map/adjoint_panel/pallas_call | solution.py:409
  50.1 0.6 %copy.9 = f32[64,256]{1,0:T(8,128)} copy(f32[64,256]{1,0:T(8,128)S(1)} %get-tuple-element.4) | data formatting | bytes 131072
  50.8 0.7 %copy.10 = f32[256,256]{1,0:T(8,128)} copy(f32[256,256]{1,0:T(8,128)S(1)} %get-tuple-element.5) | data formatting | bytes 524288
